TPU v7x, 512 devices: a whole 4x8x8 slice. The times are simulated.
512 devices in a mesh: seq: 512 (over y, x, z, core).
Axes of the slice: x: 4, y: 8, z: 8, core: 2. Of those that a mesh axis runs over, the one named last changes fastest.
Arguments:
- queries: bfloat16 [131072, 8, 128], P('seq'), may hold values from -132 to 132
- keys: bfloat16 [262144, 8, 128], P('seq'), may hold values from -6 to 6
- values: bfloat16 [262144, 8, 128], P('seq'), may hold values from -6 to 6
- routes: int32 [131072, 8], P('seq'), may hold values from 0 to 63, all different within a row; in each aligned block of 256 rows (0 to 255, 256 to 511, ...) at most 40 rows name the same one
Outputs:
- attended: bfloat16 [131072, 8, 128], P('seq')
Inputs may be any that keep to these rules, and one draw needn't show every extreme that they name: `routes`: each row names 8 different heads; among the 256 rows of one device no head is named more than 40 times, a bound that some block reaches.
All inputs are finite; a program needn't handle non-finite values.
Results may differ from a plain program's by a relative error of at most 0.0065.
Values may be sent and summed in bfloat16 or wider, within the bound.
No kernel may reach another device: no remote copies, remote signals or barrier semaphores. Data moves between devices by JAX's collectives and lax.ppermute only.
A program may use at most 64 MiB of HBM per device.

v0:
```python
import jax
import jax.numpy as jnp
from jax import lax
from jax.sharding import PartitionSpec as P

HEADS = 64
HOPS = 4
MOST = 40


def shifted(block, axis, distance):
    devices = range(lax.axis_size(axis))
    route = [(i - distance, i) for i in devices if i - distance in devices]
    return lax.ppermute(block, axis, route)


def slot_index(routes):
    flat_heads = routes.reshape(-1)
    entries = flat_heads.shape[0]
    block_rows = 128
    block_count = entries // block_rows
    heads_all = jnp.arange(HEADS, dtype=jnp.int32)
    onehot = (flat_heads[:, None] == heads_all[None, :]).astype(jnp.bfloat16)
    blocks = onehot.reshape(block_count, block_rows, HEADS)
    inner = jnp.arange(block_rows, dtype=jnp.int32)
    lower = (inner[None, :] < inner[:, None]).astype(jnp.bfloat16)
    inside_block = jnp.einsum("ab,kbh->kah", lower, blocks, preferred_element_type=jnp.float32)
    block_totals = jnp.sum(blocks.astype(jnp.float32), axis=1).astype(jnp.bfloat16)
    outer = jnp.arange(block_count, dtype=jnp.int32)
    lower_blocks = (outer[None, :] < outer[:, None]).astype(jnp.bfloat16)
    block_start = jnp.dot(lower_blocks, block_totals, preferred_element_type=jnp.float32)
    before = (inside_block + block_start[:, None, :]).reshape(entries, HEADS)
    within = jnp.sum(before * onehot.astype(jnp.float32), axis=1).astype(jnp.int32)
    return flat_heads * MOST + within


def visit(state, packed, keys_shard, values_shard, allowed):
    running, highest, denominator = state
    width = packed.shape[2]
    scores = jnp.einsum("gqd,kgd->gqk", packed, keys_shard, preferred_element_type=jnp.float32)
    scores = scores / jnp.sqrt(jnp.float32(width))
    scores = jnp.where(allowed, scores, jnp.float32(-1e30))
    newest = jnp.maximum(highest, jnp.max(scores, axis=2))
    weights = jnp.where(allowed, jnp.exp(scores - newest[:, :, None]), jnp.float32(0.0))
    factor = jnp.exp(highest - newest)
    denominator = denominator * factor + jnp.sum(weights, axis=2)
    product = jnp.einsum(
        "gqk,kgd->gqd",
        weights.astype(jnp.bfloat16),
        values_shard,
        preferred_element_type=jnp.float32,
    )
    running = running * factor[:, :, None] + product
    return (running, newest, denominator)


def shards(queries, keys, values, routes):
    tokens_count, routed_count, width = queries.shape
    context_rows, groups, _ = keys.shape
    device = lax.axis_index("seq")
    slots = slot_index(routes)
    flat = queries.reshape(-1, width)
    slot_all = jnp.arange(HEADS * MOST, dtype=jnp.int32)
    placing = (slot_all[:, None] == slots[None, :]).astype(jnp.bfloat16)
    packed = jnp.dot(placing, flat, preferred_element_type=jnp.float32).astype(jnp.bfloat16)
    tokens_of = (jnp.arange(tokens_count * routed_count, dtype=jnp.int32) // routed_count).astype(
        jnp.float32
    )
    positions = jnp.dot(placing.astype(jnp.float32), tokens_of).astype(jnp.int32)
    packed = packed.reshape(groups, -1, width)
    positions = positions.reshape(groups, -1)
    rows_group = packed.shape[1]
    offset = context_rows - tokens_count
    own_mask = (
        jnp.arange(context_rows, dtype=jnp.int32)[None, None, :] <= (positions + offset)[:, :, None]
    )
    state = (
        jnp.zeros((groups, rows_group, width), jnp.float32),
        jnp.full((groups, rows_group), -1e30, jnp.float32),
        jnp.zeros((groups, rows_group), jnp.float32),
    )
    state = visit(state, packed, keys, values, own_mask)
    moving_keys, moving_values = (keys, values)
    for travel in range(1, HOPS + 1):
        moving_keys, moving_values = shifted((moving_keys, moving_values), "seq", 1)
        usable = device - travel >= 0
        state = visit(state, packed, moving_keys, moving_values, usable)
    finished = (state[0] / state[2][:, :, None]).astype(jnp.bfloat16)
    unpacked = jnp.einsum(
        "si,sd->id", placing, finished.reshape(-1, width), preferred_element_type=jnp.float32
    )
    return unpacked.astype(jnp.bfloat16).reshape(tokens_count, routed_count, width)


def solution(mesh):
    placed = (P("seq", None, None), P("seq", None, None), P("seq", None, None), P("seq", None))
    return jax.shard_map(
        shards, mesh=mesh, in_specs=placed, out_specs=P("seq", None, None), check_vma=False
    )
```

profile of v0, /device:TPU:56, one launch (start us, length us, event | category | flops | bytes accessed | tf_op | source)
XLA Modules:
  0.0 122.9 jit_solution(16797462759061630953)
XLA Ops:
  0.0 0.0 copy-start
  0.0 1.4 %copy.11 = bf16[512,8,128]{2,0,1:T(8,128)(2,1)S(1)} copy(bf16[512,8,128]{2,1,0:T(8,128)(2,1)} %param.5) | data formatting | bytes 2097152 | tf_op args[1]
  1.4 1.9 %collective-permute-start = (bf16[512,8,128]{2,0,1:T(8,128)(2,1)S(1)}, bf16[512,8,128]{2,0,1:T(8,128)(2,1)S(1)}, u32[]{:S(2)}, u32[]{:S(2)}) collective-permute-start(bf16[512,8,128]{2,0,1:T(8,128)(2,1)S(1)} %copy.11), channel_id=1, source_target_pairs={{0,1},{1,2},{2,3},{3,4},{4,5},{5,6},{6,7},{7,8},{8,9},{9,10},{10,1... | collective-permute-start | bytes 3145736 | tf_op jit(solution)/shard_map/ppermute | solution.py:14
  3.4 2.4 %copy.12 = bf16[512,8,128]{2,0,1:T(8,128)(2,1)} copy(bf16[512,8,128]{2,1,0:T(8,128)(2,1)} %param.6) | data formatting | bytes 2097152 | tf_op args[2]
  5.8 4.4 %collective-permute-start.1 = (bf16[512,8,128]{2,0,1:T(8,128)(2,1)}, bf16[512,8,128]{2,0,1:T(8,128)(2,1)}, u32[]{:S(2)}, u32[]{:S(2)}) collective-permute-start(bf16[512,8,128]{2,0,1:T(8,128)(2,1)} %copy.12), channel_id=1, source_target_pairs={{0,1},{1,2},{2,3},{3,4},{4,5},{5,6},{6,7},{7,8},{8,9},{9,10},{10,1... | collective-permute-start | bytes 3145736 | tf_op jit(solution)/shard_map/ppermute | solution.py:14
  10.1 17.1 %collective-permute-done = bf16[512,8,128]{2,0,1:T(8,128)(2,1)S(1)} collective-permute-done((bf16[512,8,128]{2,0,1:T(8,128)(2,1)S(1)}, bf16[512,8,128]{2,0,1:T(8,128)(2,1)S(1)}, u32[]{:S(2)}, u32[]{:S(2)}) %collective-permute-start) | collective-permute-done | bytes 1048608 | tf_op jit(solution)/shard_map/ppermute | solution.py:14
  27.3 1.9 %collective-permute-start.2 = (bf16[512,8,128]{2,0,1:T(8,128)(2,1)S(1)}, bf16[512,8,128]{2,0,1:T(8,128)(2,1)S(1)}, u32[]{:S(2)}, u32[]{:S(2)}) collective-permute-start(bf16[512,8,128]{2,0,1:T(8,128)(2,1)S(1)} %collective-permute-done), channel_id=1, source_target_pairs={{0,1},{1,2},{2,3},{3,4},{4,5},{5,6},{6,7},{7,8},{8,9},{9,10},{10,1... | collective-permute-start | bytes 3145736 | tf_op jit(solution)/shard_map/ppermute | solution.py:14
  29.2 0.8 copy.10
  30.0 0.1 eq.32
  30.1 0.7 broadcast_multiply_fusion
  30.8 0.1 copy.9
  31.0 0.1 mul.84
  31.1 0.2 fusion.73
  31.3 0.1 fusion.80
  31.4 0.3 fusion.67
  31.7 6.9 %collective-permute-done.1 = bf16[512,8,128]{2,0,1:T(8,128)(2,1)} collective-permute-done((bf16[512,8,128]{2,0,1:T(8,128)(2,1)}, bf16[512,8,128]{2,0,1:T(8,128)(2,1)}, u32[]{:S(2)}, u32[]{:S(2)}) %collective-permute-start.1) | collective-permute-done | bytes 1048608 | tf_op jit(solution)/shard_map/ppermute | solution.py:14
  38.6 1.9 %collective-permute-start.3 = (bf16[512,8,128]{2,0,1:T(8,128)(2,1)}, bf16[512,8,128]{2,0,1:T(8,128)(2,1)}, u32[]{:S(2)}, u32[]{:S(2)}) collective-permute-start(bf16[512,8,128]{2,0,1:T(8,128)(2,1)} %collective-permute-done.1), channel_id=1, source_target_pairs={{0,1},{1,2},{2,3},{3,4},{4,5},{5,6},{6,7},{7,8},{8,9},{9,10},{10,1... | collective-permute-start | bytes 3145736 | tf_op jit(solution)/shard_map/ppermute | solution.py:14
  40.5 9.2 %collective-permute-done.2 = bf16[512,8,128]{2,0,1:T(8,128)(2,1)S(1)} collective-permute-done((bf16[512,8,128]{2,0,1:T(8,128)(2,1)S(1)}, bf16[512,8,128]{2,0,1:T(8,128)(2,1)S(1)}, u32[]{:S(2)}, u32[]{:S(2)}) %collective-permute-start.2) | collective-permute-done | bytes 1048608 | tf_op jit(solution)/shard_map/ppermute | solution.py:14
  49.7 1.9 %collective-permute-start.4 = (bf16[512,8,128]{2,0,1:T(8,128)(2,1)S(1)}, bf16[512,8,128]{2,0,1:T(8,128)(2,1)}, u32[]{:S(2)}, u32[]{:S(2)}) collective-permute-start(bf16[512,8,128]{2,0,1:T(8,128)(2,1)S(1)} %collective-permute-done.2), channel_id=1, source_target_pairs={{0,1},{1,2},{2,3},{3,4},{4,5},{5,6},{6,7},{7,8},{8,9},{9,10},{10,1... | collective-permute-start | bytes 3145736 | tf_op jit(solution)/shard_map/ppermute | solution.py:14
  51.7 3.4 %fusion.68 = f32[2560]{0:T(1024)S(1)} fusion(f32[2048,1]{0,1:T(1,128)S(1)} %bitcast.40, s32[2048]{0:T(1024)S(1)} %bitcast_add_fusion), kind=kOutput, calls=%fused_computation.59 | convolution fusion | flops 15728640 | bytes 26624 | tf_op jit(solution)/shard_map/dot_general | solution.py:69
  55.1 0.1 add.92
  55.2 0.0 copy-done
  55.2 0.0 copy-start.1
  55.2 3.8 %fusion.19 = bf16[2560,128]{1,0:T(8,128)(2,1)S(1)} fusion(s32[2048]{0:T(1024)S(1)} %bitcast_add_fusion, bf16[256,8,128]{2,1,0:T(8,128)(2,1)S(1)} %copy-done), kind=kOutput, calls=%fused_computation.31 | convolution fusion | flops 1347747840 | bytes 1187840 | tf_op jit(solution)/shard_map/dot_general | solution.py:65
  59.0 2.1 %collective-permute-done.3 = bf16[512,8,128]{2,0,1:T(8,128)(2,1)} collective-permute-done((bf16[512,8,128]{2,0,1:T(8,128)(2,1)}, bf16[512,8,128]{2,0,1:T(8,128)(2,1)}, u32[]{:S(2)}, u32[]{:S(2)}) %collective-permute-start.3) | collective-permute-done | bytes 1048608 | tf_op jit(solution)/shard_map/ppermute | solution.py:14
  61.1 1.9 %collective-permute-start.5 = (bf16[512,8,128]{2,0,1:T(8,128)(2,1)}, bf16[512,8,128]{2,0,1:T(8,128)(2,1)S(1)}, u32[]{:S(2)}, u32[]{:S(2)}) collective-permute-start(bf16[512,8,128]{2,0,1:T(8,128)(2,1)} %collective-permute-done.3), channel_id=1, source_target_pairs={{0,1},{1,2},{2,3},{3,4},{4,5},{5,6},{6,7},{7,8},{8,9},{9,10},{10,1... | collective-permute-start | bytes 3145736 | tf_op jit(solution)/shard_map/ppermute | solution.py:14
  63.0 0.0 copy-done.1
  63.0 1.9 %fusion.10 = (f32[8,320]{1,0:T(8,128)S(1)}, f32[8,320,512]{2,1,0:T(8,128)S(1)}) fusion(s32[8,320]{1,0:T(8,128)S(1)} %add.92, bf16[8,320,128]{2,1,0:T(8,128)(2,1)S(1)} %bitcast.35, bf16[512,8,128]{2,1,0:T(8,128)(2,1)S(1)} %copy-done.1), kind=kOutput, calls=%fused_computation.22 | convolution fusion | flops 340784640 | bytes 6967296 | tf_op jit(solution)/shard_map/gqd,kgd->gqk/dot_general | solution.py:40
  64.9 7.4 %collective-permute-done.4 = bf16[512,8,128]{2,0,1:T(8,128)(2,1)} collective-permute-done((bf16[512,8,128]{2,0,1:T(8,128)(2,1)S(1)}, bf16[512,8,128]{2,0,1:T(8,128)(2,1)}, u32[]{:S(2)}, u32[]{:S(2)}) %collective-permute-start.4) | collective-permute-done | bytes 1048608 | tf_op jit(solution)/shard_map/ppermute | solution.py:14
  72.3 1.9 %collective-permute-start.6 = (bf16[512,8,128]{2,0,1:T(8,128)(2,1)}, bf16[512,8,128]{2,0,1:T(8,128)(2,1)S(1)}, u32[]{:S(2)}, u32[]{:S(2)}) collective-permute-start(bf16[512,8,128]{2,0,1:T(8,128)(2,1)} %collective-permute-done.4), channel_id=1, source_target_pairs={{0,1},{1,2},{2,3},{3,4},{4,5},{5,6},{6,7},{7,8},{8,9},{9,10},{10,1... | collective-permute-start | bytes 3145736 | tf_op jit(solution)/shard_map/ppermute | solution.py:14
  74.2 1.0 fusion.6
  75.2 1.0 fusion.7
  76.1 7.3 %collective-permute-done.5 = bf16[512,8,128]{2,0,1:T(8,128)(2,1)S(1)} collective-permute-done((bf16[512,8,128]{2,0,1:T(8,128)(2,1)}, bf16[512,8,128]{2,0,1:T(8,128)(2,1)S(1)}, u32[]{:S(2)}, u32[]{:S(2)}) %collective-permute-start.5) | collective-permute-done | bytes 1048608 | tf_op jit(solution)/shard_map/ppermute | solution.py:14
  83.4 2.1 %collective-permute-start.7 = (bf16[512,8,128]{2,0,1:T(8,128)(2,1)S(1)}, bf16[512,8,128]{2,0,1:T(8,128)(2,1)S(1)}, u32[]{:S(2)}, u32[]{:S(2)}) collective-permute-start(bf16[512,8,128]{2,0,1:T(8,128)(2,1)S(1)} %collective-permute-done.5), channel_id=1, source_target_pairs={{0,1},{1,2},{2,3},{3,4},{4,5},{5,6},{6,7},{7,8},{8,9},{9,10},{10,1... | collective-permute-start | bytes 3145736 | tf_op jit(solution)/shard_map/ppermute | solution.py:14
  85.5 2.2 %fusion.8 = (f32[8,320]{1,0:T(8,128)S(1)}, f32[8,320,512]{2,1,0:T(8,128)S(1)}) fusion(pred[]{:T(512)S(6)} %ge.14, bf16[8,320,128]{2,1,0:T(8,128)(2,1)S(1)} %bitcast.38, bf16[512,8,128]{2,0,1:T(8,128)(2,1)} %collective-permute-done.4), kind=kOutput, calls=%fused_computation.20 | convolution fusion | flops 339473920 | bytes 6957057 | tf_op jit(solution)/shard_map/gqd,kgd->gqk/dot_general | solution.py:40
  87.7 7.0 %collective-permute-done.6 = bf16[512,8,128]{2,0,1:T(8,128)(2,1)S(1)} collective-permute-done((bf16[512,8,128]{2,0,1:T(8,128)(2,1)}, bf16[512,8,128]{2,0,1:T(8,128)(2,1)S(1)}, u32[]{:S(2)}, u32[]{:S(2)}) %collective-permute-start.6) | collective-permute-done | bytes 1048608 | tf_op jit(solution)/shard_map/ppermute | solution.py:14
  94.7 0.9 fusion.9
  95.6 2.2 %fusion.20 = f32[8,320]{1,0:T(8,128)S(1)} fusion(f32[8,320,512]{2,1,0:T(8,128)S(1)} %get-tuple-element.25, f32[8,320]{1,0:T(8,128)S(1)} %get-tuple-element.15, s32[8,320]{1,0:T(8,128)S(1)} %add.92), kind=kLoop, calls=%fused_computation.32 | loop fusion | flops 7861760 | bytes 5273600 | tf_op jit(solution)/shard_map/reduce_sum | solution.py:46
  97.9 2.9 %fusion.11 = (f32[8,320]{1,0:T(8,128)S(1)}, f32[8,320]{1,0:T(8,128)S(1)}) fusion(f32[8,320,512]{2,1,0:T(8,128)S(1)} %get-tuple-element.23, f32[8,320]{1,0:T(8,128)S(1)} %get-tuple-element.13, pred[]{:T(512)S(6)} %ge.12, f32[8,320]{1,0:T(8,128)S(1)} %get-tuple-element.12, f32[8,320,512]{2,1,0:T(8,128)S(1)} %get-tuple-element.21, pred[]{:T(512)S(6)} %ge.13), kind=kLoop, calls=%fused_computation.23 | loop fusion | flops 13102080 | bytes 10526722 | tf_op jit(solution)/shard_map/reduce_sum | solution.py:46
  100.8 0.0 copy-start.2
  100.8 2.9 %fusion.15 = (f32[8,320]{1,0:T(8,128)S(1)}, f32[8,320]{1,0:T(8,128)S(1)}) fusion(f32[8,320,512]{2,1,0:T(8,128)S(1)} %get-tuple-element.19, f32[8,320]{1,0:T(8,128)S(1)} %get-tuple-element.11, pred[]{:T(512)S(6)} %ge.14, f32[8,320]{1,0:T(8,128)S(1)} %get-tuple-element.10, f32[8,320,512]{2,1,0:T(8,128)S(1)} %get-tuple-element.17, pred[]{:T(512)S(6)} %ge.15), kind=kLoop, calls=%fused_computation.27 | loop fusion | flops 13102080 | bytes 10526722 | tf_op jit(solution)/shard_map/reduce_sum | solution.py:46
  103.8 0.0 copy-done.2
  103.8 3.0 %fusion.40 = f32[8,320,128]{2,1,0:T(8,128)S(1)} fusion(f32[8,320,512]{2,1,0:T(8,128)S(1)} %get-tuple-element.25, f32[8,320]{1,0:T(8,128)S(1)} %get-tuple-element.15, s32[8,320]{1,0:T(8,128)S(1)} %add.92, f32[8,320]{1,0:T(8,128)S(1)} %get-tuple-element.9, f32[8,320]{1,0:T(8,128)S(1)} %get-tuple-element.14, bf16[512,8,128]{2,1,0:T(8,128)(2,1)S(1)} %copy-done.2), kind=kOutput, calls=%fused_computation.45 | convolution fusion | flops 344064000 | bytes 7643136 | tf_op jit(solution)/shard_map/gqk,kgd->gqd/dot_general | solution.py:47
  106.8 2.8 %fusion.46 = f32[8,320,128]{2,1,0:T(8,128)S(1)} fusion(f32[8,320,128]{2,1,0:T(8,128)S(1)} %fusion.40, bf16[512,8,128]{2,0,1:T(8,128)(2,1)} %collective-permute-done.1, f32[8,320,512]{2,1,0:T(8,128)S(1)} %get-tuple-element.23, f32[8,320]{1,0:T(8,128)S(1)} %get-tuple-element.13, pred[]{:T(512)S(6)} %ge.12, f32[8,320]{1,0:T(8,128)S(1)} %get-tuple-element.8), kind=kOutput, calls=%fused_computation.47 | convolution fusion | flops 342753280 | bytes 8933377 | tf_op jit(solution)/shard_map/gqk,kgd->gqd/dot_general | solution.py:47
  109.6 2.8 %fusion.52 = f32[8,320,128]{2,1,0:T(8,128)S(1)} fusion(f32[8,320,128]{2,1,0:T(8,128)S(1)} %fusion.46, bf16[512,8,128]{2,0,1:T(8,128)(2,1)} %collective-permute-done.3, f32[8,320,512]{2,1,0:T(8,128)S(1)} %get-tuple-element.21, f32[8,320]{1,0:T(8,128)S(1)} %get-tuple-element.12, pred[]{:T(512)S(6)} %ge.13, f32[8,320]{1,0:T(8,128)S(1)} %get-tuple-element.7), kind=kOutput, calls=%fused_computation.49 | convolution fusion | flops 342753280 | bytes 8933377 | tf_op jit(solution)/shard_map/gqk,kgd->gqd/dot_general | solution.py:47
  112.4 2.0 %fusion.58 = f32[8,320,128]{2,1,0:T(8,128)S(1)} fusion(f32[8,320,128]{2,1,0:T(8,128)S(1)} %fusion.52, bf16[512,8,128]{2,0,1:T(8,128)(2,1)S(1)} %collective-permute-done.5, f32[8,320,512]{2,1,0:T(8,128)S(1)} %get-tuple-element.19, f32[8,320]{1,0:T(8,128)S(1)} %get-tuple-element.11, pred[]{:T(512)S(6)} %ge.14, f32[8,320]{1,0:T(8,128)S(1)} %get-tuple-element.6), kind=kOutput, calls=%fused_computation.51 | convolution fusion | flops 342753280 | bytes 8933377 | tf_op jit(solution)/shard_map/gqk,kgd->gqd/dot_general | solution.py:47
  114.5 0.0 collective-permute-done.7
  114.5 2.0 %divide_convert_fusion = bf16[8,320,128]{2,1,0:T(8,128)(2,1)S(1)} fusion(f32[8,320,128]{2,1,0:T(8,128)S(1)} %fusion.58, bf16[512,8,128]{2,0,1:T(8,128)(2,1)S(1)} %collective-permute-done.7, f32[8,320,512]{2,1,0:T(8,128)S(1)} %get-tuple-element.17, f32[8,320]{1,0:T(8,128)S(1)} %get-tuple-element.10, pred[]{:T(512)S(6)} %ge.15, f32[8,320]{1,0:T(8,128)S(1)} %get-tuple-element.5), kind=kOutput, calls=%fused_computation.53 | convolution fusion | flops 343080960 | bytes 8278017 | tf_op jit(solution)/shard_map/gqk,kgd->gqd/dot_general | solution.py:47
  116.5 6.4 %fusion.64 = bf16[256,8,128]{2,1,0:T(8,128)(2,1)} fusion(bf16[2560,128]{1,0:T(8,128)(2,1)S(1)} %bitcast.41, s32[2048]{0:T(1024)S(1)} %bitcast_add_fusion), kind=kOutput, calls=%fused_computation.54 | convolution fusion | flops 1347682304 | bytes 1187840 | tf_op jit(solution)/shard_map/si,sd->id/dot_general | solution.py:89
  (5 shorter events, 0.1 us)
Async XLA Ops:
  0.0 55.2 %copy-start = (bf16[256,8,128]{2,1,0:T(8,128)(2,1)S(1)}, bf16[256,8,128]{2,1,0:T(8,128)(2,1)}, u32[]{:S(2)}) copy-start(bf16[256,8,128]{2,1,0:T(8,128)(2,1)} %param.4) | copy-start | bytes 1572868
  1.4 25.8 %collective-permute-start = (bf16[512,8,128]{2,0,1:T(8,128)(2,1)S(1)}, bf16[512,8,128]{2,0,1:T(8,128)(2,1)S(1)}, u32[]{:S(2)}, u32[]{:S(2)}) collective-permute-start(bf16[512,8,128]{2,0,1:T(8,128)(2,1)S(1)} %copy.11), channel_id=1, source_target_pairs={{0,1},{1,2},{2,3},{3,4},{4,5},{5,6},{6,7},{7,8},{8,9},{9,10},{10,1... | collective-permute-start | bytes 3145736 | tf_op jit(solution)/shard_map/ppermute | solution.py:14
  5.8 32.9 %collective-permute-start.1 = (bf16[512,8,128]{2,0,1:T(8,128)(2,1)}, bf16[512,8,128]{2,0,1:T(8,128)(2,1)}, u32[]{:S(2)}, u32[]{:S(2)}) collective-permute-start(bf16[512,8,128]{2,0,1:T(8,128)(2,1)} %copy.12), channel_id=1, source_target_pairs={{0,1},{1,2},{2,3},{3,4},{4,5},{5,6},{6,7},{7,8},{8,9},{9,10},{10,1... | collective-permute-start | bytes 3145736 | tf_op jit(solution)/shard_map/ppermute | solution.py:14
  27.3 22.5 %collective-permute-start.2 = (bf16[512,8,128]{2,0,1:T(8,128)(2,1)S(1)}, bf16[512,8,128]{2,0,1:T(8,128)(2,1)S(1)}, u32[]{:S(2)}, u32[]{:S(2)}) collective-permute-start(bf16[512,8,128]{2,0,1:T(8,128)(2,1)S(1)} %collective-permute-done), channel_id=1, source_target_pairs={{0,1},{1,2},{2,3},{3,4},{4,5},{5,6},{6,7},{7,8},{8,9},{9,10},{10,1... | collective-permute-start | bytes 3145736 | tf_op jit(solution)/shard_map/ppermute | solution.py:14
  38.6 22.5 %collective-permute-start.3 = (bf16[512,8,128]{2,0,1:T(8,128)(2,1)}, bf16[512,8,128]{2,0,1:T(8,128)(2,1)}, u32[]{:S(2)}, u32[]{:S(2)}) collective-permute-start(bf16[512,8,128]{2,0,1:T(8,128)(2,1)} %collective-permute-done.1), channel_id=1, source_target_pairs={{0,1},{1,2},{2,3},{3,4},{4,5},{5,6},{6,7},{7,8},{8,9},{9,10},{10,1... | collective-permute-start | bytes 3145736 | tf_op jit(solution)/shard_map/ppermute | solution.py:14
  49.7 22.6 %collective-permute-start.4 = (bf16[512,8,128]{2,0,1:T(8,128)(2,1)S(1)}, bf16[512,8,128]{2,0,1:T(8,128)(2,1)}, u32[]{:S(2)}, u32[]{:S(2)}) collective-permute-start(bf16[512,8,128]{2,0,1:T(8,128)(2,1)S(1)} %collective-permute-done.2), channel_id=1, source_target_pairs={{0,1},{1,2},{2,3},{3,4},{4,5},{5,6},{6,7},{7,8},{8,9},{9,10},{10,1... | collective-permute-start | bytes 3145736 | tf_op jit(solution)/shard_map/ppermute | solution.py:14
  55.2 7.8 %copy-start.1 = (bf16[512,8,128]{2,1,0:T(8,128)(2,1)S(1)}, bf16[512,8,128]{2,1,0:T(8,128)(2,1)}, u32[]{:S(2)}) copy-start(bf16[512,8,128]{2,1,0:T(8,128)(2,1)} %param.5) | copy-start | bytes 3145732
  61.1 22.4 %collective-permute-start.5 = (bf16[512,8,128]{2,0,1:T(8,128)(2,1)}, bf16[512,8,128]{2,0,1:T(8,128)(2,1)S(1)}, u32[]{:S(2)}, u32[]{:S(2)}) collective-permute-start(bf16[512,8,128]{2,0,1:T(8,128)(2,1)} %collective-permute-done.3), channel_id=1, source_target_pairs={{0,1},{1,2},{2,3},{3,4},{4,5},{5,6},{6,7},{7,8},{8,9},{9,10},{10,1... | collective-permute-start | bytes 3145736 | tf_op jit(solution)/shard_map/ppermute | solution.py:14
  72.3 22.4 %collective-permute-start.6 = (bf16[512,8,128]{2,0,1:T(8,128)(2,1)}, bf16[512,8,128]{2,0,1:T(8,128)(2,1)S(1)}, u32[]{:S(2)}, u32[]{:S(2)}) collective-permute-start(bf16[512,8,128]{2,0,1:T(8,128)(2,1)} %collective-permute-done.4), channel_id=1, source_target_pairs={{0,1},{1,2},{2,3},{3,4},{4,5},{5,6},{6,7},{7,8},{8,9},{9,10},{10,1... | collective-permute-start | bytes 3145736 | tf_op jit(solution)/shard_map/ppermute | solution.py:14
  83.4 31.0 %collective-permute-start.7 = (bf16[512,8,128]{2,0,1:T(8,128)(2,1)S(1)}, bf16[512,8,128]{2,0,1:T(8,128)(2,1)S(1)}, u32[]{:S(2)}, u32[]{:S(2)}) collective-permute-start(bf16[512,8,128]{2,0,1:T(8,128)(2,1)S(1)} %collective-permute-done.5), channel_id=1, source_target_pairs={{0,1},{1,2},{2,3},{3,4},{4,5},{5,6},{6,7},{7,8},{8,9},{9,10},{10,1... | collective-permute-start | bytes 3145736 | tf_op jit(solution)/shard_map/ppermute | solution.py:14
  100.8 3.0 %copy-start.2 = (bf16[512,8,128]{2,1,0:T(8,128)(2,1)S(1)}, bf16[512,8,128]{2,1,0:T(8,128)(2,1)}, u32[]{:S(2)}) copy-start(bf16[512,8,128]{2,1,0:T(8,128)(2,1)} %param.6) | copy-start | bytes 3145732
where the time goes:
time: 123 us
  waiting for transfers between devices  57 us (46%)
  matrix products  33.6 us (27%)
  starting transfers between devices  17.9 us (15%)
  other arithmetic  9.09 us (7%)
  local copies, waits for them, and re-layouts  5.07 us (4%)
    ppermute x8, waiting for transfers between devices, shifted(): return lax.ppermute(block, axis, route)  57 us
    ppermute x8, starting transfers between devices, shifted(): return lax.ppermute(block, axis, route)  17.9 us
    dot_general x5, matrix products, visit(): jnp.einsum('gqk,kgd->gqd', weights.astype(jnp.bfloat16), values_shard, pr...  12.6 us
    reduce_sum x3, other arithmetic, visit(): denominator = denominator * factor + jnp.sum(weights, axis=2)  8.1 us
    dot_general x5, matrix products, visit(): jnp.einsum('gqd,kgd->gqk', packed, keys_shard, preferred_element_type=jnp...  6.91 us
    dot_general x1, matrix products, shards(): jnp.einsum('si,sd->id', placing, finished.reshape(-1, width), preferred_e...  6.41 us
    unnamed x9, local copies, waits for them, and re-layouts  4.65 us
    dot_general x1, matrix products, shards(): jnp.dot(placing, flat, preferred_element_type=jnp.float32)  3.77 us
  transfers between devices with their start and end apart: 8, of which 7 were waited for; matrix products, arithmetic and copies ran while one was open for 31% of the time, Pallas kernels for 0%

commit v1 on v0

v1 whole, which is shorter than its diff:
```python
import functools

import jax
import jax.numpy as jnp
from jax import lax
from jax.experimental import pallas as pl
from jax.experimental.pallas import tpu as pltpu
from jax.sharding import PartitionSpec as P

GROUPS = 8
MOST_GROUP = 320
ROWS = 2176
SPAN = ROWS + MOST_GROUP
META = 16
TAIL = 64
BLOCKS = ROWS // 128
CHUNK = 160
STEP = 4
LIMIT = 32 * 2**20
SMALL = pl.CostEstimate(flops=1000, bytes_accessed=1000, transcendentals=0)
LOW = -1e30
SCALE = 1.4426950408889634 / (128.0**0.5)
F32, BF16, I32 = jnp.float32, jnp.bfloat16, jnp.int32


def dot(a, b):
    return jnp.dot(a, b, preferred_element_type=F32)


def dot_t(a, b):
    return lax.dot_general(a, b, (((1,), (1,)), ((), ())), preferred_element_type=F32)


def iota(shape, dim):
    return lax.broadcasted_iota(I32, shape, dim)


def one_hot(mask):
    return jnp.where(mask, F32(1), F32(0)).astype(BF16)


def sort_kernel(routes_ref, q_ref, packed_ref, pos_ref, slots_ref, right):
    routed, tokens = routes_ref.shape
    entries = routed * tokens
    group = lax.shift_right_logical(routes_ref[...], 3)
    hot = jnp.concatenate([jnp.where(group == g, F32(1), F32(0)) for g in range(GROUPS)], axis=0)
    hot16 = hot.astype(BF16)
    before = dot(hot16, one_hot(iota((tokens, tokens), 0) < iota((tokens, tokens), 1)))
    total = dot(hot16, jnp.ones((tokens, tokens), BF16)).astype(BF16)
    side = (GROUPS * routed, GROUPS * routed)
    row, col = iota(side, 0), iota(side, 1)
    same = (row // routed) == (col // routed)
    earlier = dot(one_hot(same & (col < row)), total)
    count = dot(one_hot(same), total).astype(I32)
    sixteens = lax.shift_right_logical(count + 15, 4).astype(F32).astype(BF16)
    first = dot(one_hot(((col // routed) < (row // routed)) & (col % routed == 0)), sixteens)
    places = hot * (before + earlier + 16.0 * first)
    slots = sum(places[g * routed : (g + 1) * routed] for g in range(GROUPS)).astype(I32)
    slots_ref[...] = slots
    line = jnp.concatenate([slots[r : r + 1] for r in range(routed)], axis=1)
    right[:, :128] = q_ref[...]
    right[:, 128:] = (iota((entries, 128), 0) % tokens).astype(F32).astype(BF16)
    for b in range(BLOCKS):
        place = one_hot(iota((128, entries), 0) + b * 128 == line)
        sorted_rows = dot(place, right[...])
        packed_ref[b * 128 : (b + 1) * 128] = sorted_rows[:, :128].astype(BF16)
        pos_ref[b * 128 : (b + 1) * 128] = sorted_rows[:, 128:].astype(BF16)
    starts = jnp.concatenate([first[g * routed : g * routed + 1, :128] for g in range(GROUPS)], axis=0)
    packed_ref[ROWS : ROWS + META] = jnp.concatenate([starts, jnp.zeros_like(starts)], axis=0).astype(BF16)


def sort_queries(routes_t, queries_r):
    routed, tokens = routes_t.shape
    return pl.pallas_call(
        sort_kernel,
        out_shape=[
            jax.ShapeDtypeStruct((ROWS + META, 128), BF16),
            jax.ShapeDtypeStruct((ROWS, 128), BF16),
            jax.ShapeDtypeStruct((routed, tokens), I32),
        ],
        scratch_shapes=[pltpu.VMEM((routed * tokens, 256), BF16)],
        compiler_params=pltpu.CompilerParams(vmem_limit_bytes=24 * 2**20),
        cost_estimate=SMALL,
        name="sort_queries",
    )(routes_t, queries_r)


def attend_kernel(kind, info, q_ref, *refs):
    kv_count = {"own": 2, "near": 3, "far": 2}[kind]
    kv = refs[:kv_count]
    refs = refs[kv_count:]
    if kind == "own":
        pos_ref, out_ref, lse_ref, qs, os, ls, ps = refs
    else:
        out_ref, qs, os, ls, tail = refs
    step = pl.program_id(0)
    odd, chip = info[8], info[9]

    def shard_parts(i, most):
        first = [(kv[0][0, i], kv[0][1, i], None, False)]
        second = [(kv[1][0, i], kv[1][1, i], None, False)]
        if kind == "own":
            first = [
                (kv[0][0, i, :256], kv[0][1, i, :256], None, False),
                (kv[0][0, i, 256:], kv[0][1, i, 256:], None, True),
            ]
        if kind == "near" and most == 3:
            flag = jnp.where(chip >= 1, F32(0), F32(LOW))
            second.append((kv[2][0, i], kv[2][1, i], flag, False))
        return first if most == 1 else first + second

    def work(most):
        @pl.when(step == 0)
        def _():
            qs[:ROWS] = q_ref[:ROWS]
            os[...] = jnp.zeros_like(os)
            ls[...] = jnp.zeros_like(ls)
            if kind == "own":
                ps[:ROWS] = pos_ref[...]

        units = []
        for i in range(STEP):
            start = pl.multiple_of(info[step * STEP + i] * 16, 16)
            parts = shard_parts(i, most)
            for c in range(MOST_GROUP // CHUNK):
                units.append((pl.ds(pl.multiple_of(start + c * CHUNK, 16), CHUNK), parts))
        scored = []
        for rows, parts in units:
            q = qs[rows, :]
            scores = []
            for k, _, _, causal in parts:
                s = dot_t(q, k)
                if causal:
                    reach = ps[rows, :].astype(F32)[:, :1]
                    s = jnp.where(iota(s.shape, 1).astype(F32) <= reach, s, F32(LOW))
                scores.append(s)
            scored.append(scores)
        tops = []
        for (rows, parts), scores in zip(units, scored):
            peaks = []
            for s, (_, _, bias, _) in zip(scores, parts):
                peak = jnp.max(s, axis=1, keepdims=True)
                peaks.append(peak if bias is None else peak + bias)
            tops.append(functools.reduce(jnp.maximum, peaks))
        results = []
        for (rows, parts), scores, top in zip(units, scored, tops):
            both = None
            for s, (_, v, bias, _) in zip(scores, parts):
                base = top if bias is None else top - bias
                weight = jnp.exp2((s - base) * F32(SCALE)).astype(BF16)
                product = dot(weight, jnp.concatenate([v, jnp.ones_like(v)], axis=1))
                both = product if both is None else both + product
            results.append(both)
        for (rows, parts), both, top in zip(units, results, tops):
            total = both[:, 128:]
            os[rows, :] = (both[:, :128] / total).astype(BF16)
            ls[rows, :] = top * F32(SCALE) + jnp.log2(total)

        @pl.when(step == GROUPS // STEP - 1)
        def _():
            out_ref[:ROWS] = os[:ROWS]
            if kind == "own":
                lse_ref[...] = ls[:ROWS]
            else:
                eye = iota((128, 128), 0) == iota((128, 128), 1)
                tail[...] = jnp.zeros_like(tail)
                for b in range(BLOCKS):
                    square = ls[b * 128 : (b + 1) * 128]
                    line = jnp.sum(jnp.where(eye, square, F32(0)), axis=0, keepdims=True)
                    high = line.astype(BF16).astype(F32)
                    middle = (line - high).astype(BF16).astype(F32)
                    tail[b : b + 1] = high
                    tail[BLOCKS + b : BLOCKS + b + 1] = middle
                    tail[2 * BLOCKS + b : 2 * BLOCKS + b + 1] = line - high - middle
                out_ref[ROWS:] = tail[...].astype(BF16)

    even_most, odd_most = {"own": (1, 2), "near": (2, 3), "far": (2, 0)}[kind]
    pl.when(odd == 0)(lambda: work(even_most))
    if odd_most:
        pl.when(odd == 1)(lambda: work(odd_most))


def attend(kind, info, packed, kvs, pos=None):
    kv_spec = pl.BlockSpec((2, STEP, 512, 128), lambda g: (0, g, 0, 0))

    def whole(rows):
        return pl.BlockSpec((rows, 128), lambda g: (0, 0))

    in_specs = [pl.BlockSpec(memory_space=pltpu.SMEM), whole(ROWS + META)] + [kv_spec] * len(kvs)
    args = [info, packed, *kvs]
    scratch = [pltpu.VMEM((SPAN, 128), BF16), pltpu.VMEM((SPAN, 128), BF16), pltpu.VMEM((SPAN, 128), F32)]
    if kind == "own":
        in_specs.append(whole(ROWS))
        args.append(pos)
        out_shape = [jax.ShapeDtypeStruct((ROWS, 128), BF16), jax.ShapeDtypeStruct((ROWS, 128), F32)]
        out_specs = [whole(ROWS), whole(ROWS)]
        scratch.append(pltpu.VMEM((SPAN, 128), BF16))
    else:
        out_shape = jax.ShapeDtypeStruct((ROWS + TAIL, 128), BF16)
        out_specs = whole(ROWS + TAIL)
        scratch.append(pltpu.VMEM((TAIL, 128), F32))
    return pl.pallas_call(
        functools.partial(attend_kernel, kind),
        grid=(GROUPS // STEP,),
        in_specs=in_specs,
        out_specs=out_specs,
        out_shape=out_shape,
        scratch_shapes=scratch,
        compiler_params=pltpu.CompilerParams(
            dimension_semantics=("arbitrary",), vmem_limit_bytes=LIMIT
        ),
        cost_estimate=SMALL,
        name="attend_" + kind,
    )(*args)


def finish_kernel(info, own_ref, lse_ref, near_ref, far_ref, slots_ref, out_ref, merged):
    odd, chip = info[8], info[9]
    near_on = chip >= 1
    far_on = (chip >= 2) & (odd == 0)
    eye = iota((128, 128), 0) == iota((128, 128), 1)

    def lines(ref):
        tail = ref[ROWS:].astype(F32)
        return tail[:BLOCKS] + tail[BLOCKS : 2 * BLOCKS] + tail[2 * BLOCKS : 3 * BLOCKS]

    near_lines, far_lines = lines(near_ref), lines(far_ref)
    for b in range(BLOCKS):
        rows = slice(b * 128, (b + 1) * 128)
        own = lse_ref[rows]

        def column(table, on):
            picked = jnp.where(eye, table[b : b + 1], F32(0))
            return jnp.where(on, jnp.sum(picked, axis=1, keepdims=True), F32(LOW))

        near, far = column(near_lines, near_on), column(far_lines, far_on)
        top = jnp.maximum(own, jnp.maximum(near, far))
        a, n, f = jnp.exp2(own - top), jnp.exp2(near - top), jnp.exp2(far - top)
        mixed = a * own_ref[rows].astype(F32) + n * near_ref[rows].astype(F32) + f * far_ref[rows].astype(F32)
        merged[rows] = (mixed / (a + n + f)).astype(BF16)
    entries = out_ref.shape[0]
    for e in range(entries // 256):
        rows = slice(e * 256, (e + 1) * 256)
        place = one_hot(iota((256, ROWS), 1) == slots_ref[rows])
        out_ref[rows] = dot(place, merged[...]).astype(BF16)


def finish(info, own, lse, near, far, slots_column):
    entries = slots_column.shape[0]
    return pl.pallas_call(
        finish_kernel,
        in_specs=[pl.BlockSpec(memory_space=pltpu.SMEM)] + [pl.BlockSpec(memory_space=pltpu.VMEM)] * 5,
        out_shape=jax.ShapeDtypeStruct((entries, 128), BF16),
        scratch_shapes=[pltpu.VMEM((ROWS, 128), BF16)],
        compiler_params=pltpu.CompilerParams(vmem_limit_bytes=24 * 2**20),
        cost_estimate=SMALL,
        name="finish",
    )(info, own, lse, near, far, slots_column)


def moved(block, distance, sources=lambda i: True):
    devices = range(lax.axis_size("seq"))
    return lax.ppermute(
        block, "seq", [(i, i + distance) for i in devices if sources(i) and i + distance in devices]
    )


def odd_device(i):
    return i % 2 == 1


def even_device(i):
    return i % 2 == 0


def shards(queries, keys, values, routes):
    tokens, routed, width = queries.shape
    devices = range(lax.axis_size("seq"))
    device = lax.axis_index("seq").astype(I32)
    flags = jnp.stack([device % 2, device // 2])

    def info(packed):
        return jnp.concatenate([packed[ROWS : ROWS + 8, 0].astype(I32), flags])

    def after(x, *others):
        return lax.optimization_barrier((x, *others))[0]

    kv = jnp.stack([keys.transpose(1, 0, 2), values.transpose(1, 0, 2)])
    kv_forward = moved(kv, 2, odd_device)
    packed, pos, slots = sort_queries(after(routes.T, kv), queries.transpose(1, 0, 2).reshape(-1, width))
    column = slots.T.reshape(-1, 1)
    own_info = info(packed)
    far_q = moved(packed, -4, even_device)
    kv_sibling = lax.ppermute(after(kv, packed), "seq", [(i, i ^ 1) for i in devices])
    own, lse = attend("own", own_info, packed, [kv, kv_sibling], pos)
    near_q = moved(after(packed, own, column), -2)
    far_q = after(far_q, own)
    far_out = attend("far", info(far_q), far_q, [kv, kv_sibling])
    far_back = moved(far_out, 4, even_device)
    near_q = after(near_q, far_out)
    near_back = moved(attend("near", info(near_q), near_q, [kv, kv_sibling, kv_forward]), 2)
    out = finish(own_info, own, lse, near_back, far_back, column)
    return out.reshape(tokens, routed, width)


def solution(mesh):
    placed = (P("seq", None, None), P("seq", None, None), P("seq", None, None), P("seq", None))
    return jax.shard_map(
        shards, mesh=mesh, in_specs=placed, out_specs=P("seq", None, None), check_vma=False
    )
```

time: 123 us -> 88.2 us (0.72)
  the two profiles are of different devices: /device:TPU:56 before, /device:TPU:57 now
where the time goes in v1:
time: 88.2 us; the launch traced here: 87.7 us
  waiting for transfers between devices  31.3 us (35%)
  Pallas kernels  24.7 us (28%)
  starting transfers between devices  23 us (26%)
  local copies, waits for them, and re-layouts  6.35 us (7%)
  other arithmetic  2.13 us (2%)
    ppermute x5, waiting for transfers between devices, moved(): lax.ppermute(block, 'seq', [(i, i + distance) for i in devices if sources...  31.3 us
    ppermute x5, starting transfers between devices, moved(): lax.ppermute(block, 'seq', [(i, i + distance) for i in devices if sources...  20.5 us
    pallas_call x3, Pallas kernels, attend(): pl.pallas_call(functools.partial(attend_kernel, kind), grid=(GROUPS // ST...  15.4 us
    pallas_call x1, Pallas kernels, finish(): pl.pallas_call(finish_kernel, in_specs=[pl.BlockSpec(memory_space=pltpu.S...  5.43 us
    pallas_call x1, Pallas kernels, sort_queries(): pl.pallas_call(sort_kernel, out_shape=[jax.ShapeDtypeStruct((ROWS + META,...  3.88 us
    unnamed x12, local copies, waits for them, and re-layouts  3.76 us
    ppermute x1, starting transfers between devices, shards(): lax.ppermute(after(kv, packed), 'seq', [(i, i ^ 1) for i in devices])  2.57 us
    another operation x1, local copies, waits for them, and re-layouts, shards(): kv = jnp.stack([keys.transpose(1, 0, 2), values.transpose(1, 0, 2)])  1.92 us
  transfers between devices with their start and end apart: 6, of which 2 were waited for; matrix products, arithmetic and copies ran while one was open for 3% of the time, Pallas kernels for 18%

profile of v1, /device:TPU:57, one launch (start us, length us, event | category | flops | bytes accessed | tf_op | source)
XLA Modules:
  0.0 87.7 jit_solution(13227949887427357779)
XLA Ops:
  0.0 1.9 %copy_bitcast_fusion = (bf16[1,8,512,128]{3,2,1,0:T(8,128)(2,1)S(1)}, bf16[1,8,512,128]{3,2,1,0:T(8,128)(2,1)S(1)}) fusion(bf16[512,8,128]{2,1,0:T(8,128)(2,1)} %param.6, bf16[512,8,128]{2,1,0:T(8,128)(2,1)} %param.5), kind=kLoop, calls=%fused_computation.1 | loop fusion | bytes 4194304 | tf_op jit(solution)/shard_map/stack | solution.py:288
  1.9 0.0 copy-start.5
  1.9 0.0 copy-start.4
  2.0 0.2 pad_maximum_fusion.refs_0_
  2.2 0.8 copy-done.5
  3.0 0.1 copy.11
  3.0 0.0 copy-done.4
  3.1 3.9 %sort_queries.1 = (bf16[2192,128]{1,0:T(8,128)(2,1)}, bf16[2176,128]{1,0:T(8,128)(2,1)S(1)}, s32[8,256]{1,0:T(8,128)S(1)}) custom-call(s32[8,256]{1,0:T(8,128)S(1)} %bitcast.16, bf16[2048,128]{1,0:T(8,128)(2,1)S(1)} %bitcast.15), custom_call_target="tpu_custom_call" | custom-call | flops 1000 | bytes 1000 | tf_op jit(solution)/shard_map/sort_queries/pallas_call | solution.py:74
  6.9 0.0 copy-start
  6.9 0.8 copy-done
  7.8 2.6 %collective-permute-start = (bf16[2,8,512,128]{3,2,1,0:T(8,128)(2,1)S(1)}, bf16[2,8,512,128]{3,2,1,0:T(8,128)(2,1)}, u32[]{:S(2)}, u32[]{:S(2)}) collective-permute-start(bf16[2,8,512,128]{3,2,1,0:T(8,128)(2,1)S(1)} %pad_maximum_fusion.refs_0_), channel_id=1, source_target_pairs={{0,1},{1,0},{2,3},{3,2},{4,5},{5,4},{6,7},{7,6},{8,9},{9,8},{10,11... | collective-permute-start | bytes 6291464 | tf_op jit(solution)/shard_map/ppermute | solution.py:294
  10.3 4.0 %collective-permute-start.3 = (bf16[2,8,512,128]{3,2,1,0:T(8,128)(2,1)S(1)}, bf16[2,8,512,128]{3,2,1,0:T(8,128)(2,1)}, u32[]{:S(2)}, u32[]{:S(2)}) collective-permute-start(bf16[2,8,512,128]{3,2,1,0:T(8,128)(2,1)S(1)} %pad_maximum_fusion.refs_0_), channel_id=1, source_target_pairs={{1,3},{3,5},{5,7},{7,9},{9,11},{11,13},{13,15},{15,17},{17,19},{19... | collective-permute-start | bytes 6291464 | tf_op jit(solution)/shard_map/ppermute | solution.py:263
  14.3 1.5 %collective-permute-start.2 = (bf16[2192,128]{1,0:T(8,128)(2,1)}, bf16[2192,128]{1,0:T(8,128)(2,1)}, u32[]{:S(2)}, u32[]{:S(2)}) collective-permute-start(bf16[2192,128]{1,0:T(8,128)(2,1)} %get-tuple-element.22.q_ref), channel_id=1, source_target_pairs={{4,0},{6,2},{8,4},{10,6},{12,8},{14,10},{16,12},{18,14},{20,16},{2... | collective-permute-start | bytes 1683464 | tf_op jit(solution)/shard_map/ppermute | solution.py:263
  15.8 0.1 copy.12
  16.0 0.1 reshape.16
  16.1 0.8 convert_reduce_fusion.2
  16.9 0.1 add_add_fusion.info
  17.0 0.0 collective-permute-done.refs_1_
  17.0 0.0 copy-start.1
  17.0 1.1 %copy-done.1 = bf16[2176,128]{1,0:T(8,128)(2,1)S(1)} copy-done((bf16[2176,128]{1,0:T(8,128)(2,1)S(1)}, bf16[2176,128]{1,0:T(8,128)(2,1)}, u32[]{:S(2)}) %copy-start.1) | copy-done | bytes 557080
  18.0 5.3 %attend_own.1 = (bf16[2176,128]{1,0:T(8,128)(2,1)S(1)}, f32[2176,128]{1,0:T(8,128)S(1)}) custom-call(s32[10]{0:T(128)S(1)} %add_add_fusion.info, bf16[2192,128]{1,0:T(8,128)(2,1)} %get-tuple-element.22.q_ref, bf16[2,8,512,128]{3,2,1,0:T(8,128)(2,1)S(1)} %pad_maximum_fusion.refs_0_, bf16[2,8,512,128]{3,2,1,0:T(8,128)(2,1)} %collective-permute-done.refs_1_, ...), custom_call_target="tpu_custom_call" | custom-call | flops 1000 | bytes 1000 | tf_op jit(solution)/shard_map/attend_own/pallas_call | solution.py:202
  23.3 0.0 copy-start.2
  23.3 11.6 %collective-permute-start.1 = (bf16[2192,128]{1,0:T(8,128)(2,1)}, bf16[2192,128]{1,0:T(8,128)(2,1)S(1)}, u32[]{:S(2)}, u32[]{:S(2)}) collective-permute-start(bf16[2192,128]{1,0:T(8,128)(2,1)} %get-tuple-element.22.q_ref), channel_id=1, source_target_pairs={{2,0},{3,1},{4,2},{5,3},{6,4},{7,5},{8,6},{9,7},{10,8},{11,9},{12,... | collective-permute-start | bytes 1683464 | tf_op jit(solution)/shard_map/ppermute | solution.py:263
  34.9 0.0 collective-permute-done.2.q_ref
  34.9 0.8 convert_reduce_fusion.1
  35.7 0.1 add_add_fusion.1.info
  35.8 2.6 %attend_far.1 = bf16[2240,128]{1,0:T(8,128)(2,1)} custom-call(s32[10]{0:T(128)S(1)} %add_add_fusion.1.info, bf16[2192,128]{1,0:T(8,128)(2,1)} %collective-permute-done.2.q_ref, bf16[2,8,512,128]{3,2,1,0:T(8,128)(2,1)S(1)} %pad_maximum_fusion.refs_0_, bf16[2,8,512,128]{3,2,1,0:T(8,128)(2,1)} %collective-permute-done.refs_1_), custom_call_target="tpu_custom_call" | custom-call | flops 1000 | bytes 1000 | tf_op jit(solution)/shard_map/attend_far/pallas_call | solution.py:202
  38.5 0.0 copy-done.2
  38.5 1.5 %collective-permute-start.5 = (bf16[2240,128]{1,0:T(8,128)(2,1)}, bf16[2240,128]{1,0:T(8,128)(2,1)}, u32[]{:S(2)}, u32[]{:S(2)}) collective-permute-start(bf16[2240,128]{1,0:T(8,128)(2,1)} %attend_far.1), channel_id=1, source_target_pairs={{0,4},{2,6},{4,8},{6,10},{8,12},{10,14},{12,16},{14,18},{16,20},{1... | collective-permute-start | bytes 1720328 | tf_op jit(solution)/shard_map/ppermute | solution.py:263
  39.9 10.5 %collective-permute-done.1.q_ref = bf16[2192,128]{1,0:T(8,128)(2,1)S(1)} collective-permute-done((bf16[2192,128]{1,0:T(8,128)(2,1)}, bf16[2192,128]{1,0:T(8,128)(2,1)S(1)}, u32[]{:S(2)}, u32[]{:S(2)}) %collective-permute-start.1) | collective-permute-done | bytes 561184 | tf_op jit(solution)/shard_map/ppermute | solution.py:263
  50.5 0.1 convert_reduce_fusion
  50.6 0.1 add_add_fusion.2.info
  50.7 0.0 collective-permute-done.3.refs_2_
  50.7 7.5 %attend_near.1 = bf16[2240,128]{1,0:T(8,128)(2,1)} custom-call(s32[10]{0:T(128)S(1)} %add_add_fusion.2.info, bf16[2192,128]{1,0:T(8,128)(2,1)S(1)} %collective-permute-done.1.q_ref, bf16[2,8,512,128]{3,2,1,0:T(8,128)(2,1)S(1)} %pad_maximum_fusion.refs_0_, bf16[2,8,512,128]{3,2,1,0:T(8,128)(2,1)} %collective-permute-done.refs_1_, ...), custom_call_target="tpu_custom_call" | custom-call | flops 1000 | bytes 1000 | tf_op jit(solution)/shard_map/attend_near/pallas_call | solution.py:202
  58.2 1.9 %collective-permute-start.4 = (bf16[2240,128]{1,0:T(8,128)(2,1)}, bf16[2240,128]{1,0:T(8,128)(2,1)S(1)}, u32[]{:S(2)}, u32[]{:S(2)}) collective-permute-start(bf16[2240,128]{1,0:T(8,128)(2,1)} %attend_near.1), channel_id=1, source_target_pairs={{0,2},{1,3},{2,4},{3,5},{4,6},{5,7},{6,8},{7,9},{8,10},{9,11},{10,... | collective-permute-start | bytes 1720328 | tf_op jit(solution)/shard_map/ppermute | solution.py:263
  60.1 0.4 copy.13.slots_ref
  60.4 0.0 collective-permute-done.5.far_ref
  60.5 20.7 %collective-permute-done.4.near_ref = bf16[2240,128]{1,0:T(8,128)(2,1)S(1)} collective-permute-done((bf16[2240,128]{1,0:T(8,128)(2,1)}, bf16[2240,128]{1,0:T(8,128)(2,1)S(1)}, u32[]{:S(2)}, u32[]{:S(2)}) %collective-permute-start.4) | collective-permute-done | bytes 573472 | tf_op jit(solution)/shard_map/ppermute | solution.py:263
  81.2 0.0 copy-start.3
  81.2 1.1 %copy-done.3 = bf16[2176,128]{1,0:T(8,128)(2,1)S(1)} copy-done((bf16[2176,128]{1,0:T(8,128)(2,1)S(1)}, bf16[2176,128]{1,0:T(8,128)(2,1)}, u32[]{:S(2)}) %copy-start.3) | copy-done | bytes 557080
  82.3 5.4 %finish.1 = bf16[2048,128]{1,0:T(8,128)(2,1)} custom-call(s32[10]{0:T(128)S(1)} %add_add_fusion.info, bf16[2176,128]{1,0:T(8,128)(2,1)S(1)} %copy-done.3, f32[2176,128]{1,0:T(8,128)S(1)} %get-tuple-element.20.lse_ref, bf16[2240,128]{1,0:T(8,128)(2,1)S(1)} %collective-permute-done.4.near_ref, bf16[2240,128]{1,0:T(8,128)(2,1)} %collective-permute-done.5.far_ref, ...), custom_call_target="tpu_custom_call" | custom-call | flops 1000 | bytes 1000 | tf_op jit(solution)/shard_map/finish/pallas_call | solution.py:250
Async XLA Ops:
  1.9 1.0 %copy-start.5 = (bf16[256,8,128]{2,1,0:T(8,128)(2,1)S(1)}, bf16[256,8,128]{2,1,0:T(8,128)(2,1)}, u32[]{:S(2)}) copy-start(bf16[256,8,128]{2,1,0:T(8,128)(2,1)} %param.4) | copy-start | bytes 1572868
  1.9 1.1 %copy-start.4 = (s32[256,8]{0,1:T(8,128)S(1)}, s32[256,8]{0,1:T(8,128)}, u32[]{:S(2)}) copy-start(s32[256,8]{0,1:T(8,128)} %param.7) | copy-start | bytes 24580
  6.9 0.8 copy-start
  7.8 9.2 %collective-permute-start = (bf16[2,8,512,128]{3,2,1,0:T(8,128)(2,1)S(1)}, bf16[2,8,512,128]{3,2,1,0:T(8,128)(2,1)}, u32[]{:S(2)}, u32[]{:S(2)}) collective-permute-start(bf16[2,8,512,128]{3,2,1,0:T(8,128)(2,1)S(1)} %pad_maximum_fusion.refs_0_), channel_id=1, source_target_pairs={{0,1},{1,0},{2,3},{3,2},{4,5},{5,4},{6,7},{7,6},{8,9},{9,8},{10,11... | collective-permute-start | bytes 6291464 | tf_op jit(solution)/shard_map/ppermute | solution.py:294
  10.3 40.3 %collective-permute-start.3 = (bf16[2,8,512,128]{3,2,1,0:T(8,128)(2,1)S(1)}, bf16[2,8,512,128]{3,2,1,0:T(8,128)(2,1)}, u32[]{:S(2)}, u32[]{:S(2)}) collective-permute-start(bf16[2,8,512,128]{3,2,1,0:T(8,128)(2,1)S(1)} %pad_maximum_fusion.refs_0_), channel_id=1, source_target_pairs={{1,3},{3,5},{5,7},{7,9},{9,11},{11,13},{13,15},{15,17},{17,19},{19... | collective-permute-start | bytes 6291464 | tf_op jit(solution)/shard_map/ppermute | solution.py:263
  14.3 20.6 %collective-permute-start.2 = (bf16[2192,128]{1,0:T(8,128)(2,1)}, bf16[2192,128]{1,0:T(8,128)(2,1)}, u32[]{:S(2)}, u32[]{:S(2)}) collective-permute-start(bf16[2192,128]{1,0:T(8,128)(2,1)} %get-tuple-element.22.q_ref), channel_id=1, source_target_pairs={{4,0},{6,2},{8,4},{10,6},{12,8},{14,10},{16,12},{18,14},{20,16},{2... | collective-permute-start | bytes 1683464 | tf_op jit(solution)/shard_map/ppermute | solution.py:263
  17.0 1.1 %copy-start.1 = (bf16[2176,128]{1,0:T(8,128)(2,1)S(1)}, bf16[2176,128]{1,0:T(8,128)(2,1)}, u32[]{:S(2)}) copy-start(bf16[2176,128]{1,0:T(8,128)(2,1)} %copy-done) | copy-start | bytes 1671172
  23.3 15.1 %copy-start.2 = (bf16[2176,128]{1,0:T(8,128)(2,1)}, bf16[2176,128]{1,0:T(8,128)(2,1)S(1)}, u32[]{:S(2)}) copy-start(bf16[2176,128]{1,0:T(8,128)(2,1)S(1)} %get-tuple-element.19.own_ref) | copy-start | bytes 1671172
  23.3 27.1 %collective-permute-start.1 = (bf16[2192,128]{1,0:T(8,128)(2,1)}, bf16[2192,128]{1,0:T(8,128)(2,1)S(1)}, u32[]{:S(2)}, u32[]{:S(2)}) collective-permute-start(bf16[2192,128]{1,0:T(8,128)(2,1)} %get-tuple-element.22.q_ref), channel_id=1, source_target_pairs={{2,0},{3,1},{4,2},{5,3},{6,4},{7,5},{8,6},{9,7},{10,8},{11,9},{12,... | collective-permute-start | bytes 1683464 | tf_op jit(solution)/shard_map/ppermute | solution.py:263
  38.5 22.0 %collective-permute-start.5 = (bf16[2240,128]{1,0:T(8,128)(2,1)}, bf16[2240,128]{1,0:T(8,128)(2,1)}, u32[]{:S(2)}, u32[]{:S(2)}) collective-permute-start(bf16[2240,128]{1,0:T(8,128)(2,1)} %attend_far.1), channel_id=1, source_target_pairs={{0,4},{2,6},{4,8},{6,10},{8,12},{10,14},{12,16},{14,18},{16,20},{1... | collective-permute-start | bytes 1720328 | tf_op jit(solution)/shard_map/ppermute | solution.py:263
  58.2 23.0 %collective-permute-start.4 = (bf16[2240,128]{1,0:T(8,128)(2,1)}, bf16[2240,128]{1,0:T(8,128)(2,1)S(1)}, u32[]{:S(2)}, u32[]{:S(2)}) collective-permute-start(bf16[2240,128]{1,0:T(8,128)(2,1)} %attend_near.1), channel_id=1, source_target_pairs={{0,2},{1,3},{2,4},{3,5},{4,6},{5,7},{6,8},{7,9},{8,10},{9,11},{10,... | collective-permute-start | bytes 1720328 | tf_op jit(solution)/shard_map/ppermute | solution.py:263
  81.2 1.1 %copy-start.3 = (bf16[2176,128]{1,0:T(8,128)(2,1)S(1)}, bf16[2176,128]{1,0:T(8,128)(2,1)}, u32[]{:S(2)}) copy-start(bf16[2176,128]{1,0:T(8,128)(2,1)} %copy-done.2) | copy-start | bytes 1671172

commit v2 on v1

v2 whole, which is shorter than its diff:
```python
import functools

import jax
import jax.numpy as jnp
from jax import lax
from jax.experimental import pallas as pl
from jax.experimental.pallas import tpu as pltpu
from jax.sharding import PartitionSpec as P

GROUPS = 8
MOST_GROUP = 320
ROWS = 2176
SPAN = ROWS + MOST_GROUP
META = 16
TAIL = 64
BLOCKS = ROWS // 128
LINES = 24
CHUNK = 160
STEP = 4
LIMIT = 32 * 2**20
SMALL = pl.CostEstimate(flops=1000, bytes_accessed=1000, transcendentals=0)
LOW = -1e30
SCALE = 1.4426950408889634 / (128.0**0.5)
F32, BF16, I32 = jnp.float32, jnp.bfloat16, jnp.int32


def dot(a, b):
    return jnp.dot(a, b, preferred_element_type=F32)


def dot_t(a, b):
    return lax.dot_general(a, b, (((1,), (1,)), ((), ())), preferred_element_type=F32)


def iota(shape, dim):
    return lax.broadcasted_iota(I32, shape, dim)


def one_hot(mask):
    return jnp.where(mask, F32(1), F32(0)).astype(BF16)


def sort_kernel(routes_ref, q_ref, packed_ref, pos_ref, slots_ref, right):
    routed, tokens = routes_ref.shape
    entries = routed * tokens
    group = lax.shift_right_logical(routes_ref[...], 3)
    hot = jnp.concatenate([jnp.where(group == g, F32(1), F32(0)) for g in range(GROUPS)], axis=0)
    hot16 = hot.astype(BF16)
    before = dot(hot16, one_hot(iota((tokens, tokens), 0) < iota((tokens, tokens), 1)))
    total = dot(hot16, jnp.ones((tokens, tokens), BF16)).astype(BF16)
    side = (GROUPS * routed, GROUPS * routed)
    row, col = iota(side, 0), iota(side, 1)
    same = (row // routed) == (col // routed)
    earlier = dot(one_hot(same & (col < row)), total)
    count = dot(one_hot(same), total).astype(I32)
    sixteens = lax.shift_right_logical(count + 15, 4).astype(F32).astype(BF16)
    first = dot(one_hot(((col // routed) < (row // routed)) & (col % routed == 0)), sixteens)
    places = hot * (before + earlier + 16.0 * first)
    slots = sum(places[g * routed : (g + 1) * routed] for g in range(GROUPS)).astype(I32)
    slots_ref[...] = slots
    line = jnp.concatenate([slots[r : r + 1] for r in range(routed)], axis=1)
    right[:, :128] = q_ref[...]
    right[:, 128:] = (iota((entries, 128), 0) % tokens).astype(F32).astype(BF16)
    eye = iota((128, 128), 0) == iota((128, 128), 1)
    pos_ref[...] = jnp.zeros_like(pos_ref)
    for b in range(BLOCKS):
        place = one_hot(iota((128, entries), 0) + b * 128 == line)
        sorted_rows = dot(place, right[...])
        packed_ref[b * 128 : (b + 1) * 128] = sorted_rows[:, :128].astype(BF16)
        pos_ref[b : b + 1] = jnp.sum(jnp.where(eye, sorted_rows[:, 128:], F32(0)), axis=0, keepdims=True)
    starts = jnp.concatenate([first[g * routed : g * routed + 1, :128] for g in range(GROUPS)], axis=0)
    packed_ref[ROWS : ROWS + META] = jnp.concatenate([starts, jnp.zeros_like(starts)], axis=0).astype(BF16)


def sort_queries(routes_t, queries_r):
    routed, tokens = routes_t.shape
    return pl.pallas_call(
        sort_kernel,
        out_shape=[
            jax.ShapeDtypeStruct((ROWS + META, 128), BF16),
            jax.ShapeDtypeStruct((LINES, 128), F32),
            jax.ShapeDtypeStruct((routed, tokens), I32),
        ],
        scratch_shapes=[pltpu.VMEM((routed * tokens, 256), BF16)],
        compiler_params=pltpu.CompilerParams(vmem_limit_bytes=24 * 2**20),
        cost_estimate=SMALL,
        name="sort_queries",
    )(routes_t, queries_r)


def attend_kernel(kind, flags, *refs):
    q_count, kv_count = {"own": (1, 1), "near": (1, 3), "far": (2, 2)}[kind]
    q_refs, refs = refs[:q_count], refs[q_count:]
    kv, refs = refs[:kv_count], refs[kv_count:]
    if kind == "own":
        pos_ref, out_ref, qs, os, ls, tail, starts, ps = refs
    else:
        out_ref, qs, os, ls, tail, starts = refs
    step = pl.program_id(0)
    odd, chip = flags[0], flags[1]

    def shard_parts(i, is_odd):
        if kind == "own":
            return [
                (kv[0][0, i, :256], kv[0][1, i, :256], None, False),
                (kv[0][0, i, 256:], kv[0][1, i, 256:], None, True),
            ]
        sibling = (kv[1][0, i], kv[1][1, i], None, False)
        if kind == "far" and is_odd:
            return [sibling]
        parts = [(kv[0][0, i], kv[0][1, i], None, False), sibling]
        if is_odd:
            flag = jnp.where(chip >= 1, F32(0), F32(LOW))
            parts.append((kv[2][0, i], kv[2][1, i], flag, False))
        return parts

    def work(is_odd):
        @pl.when(step == 0)
        def _():
            if kind == "far" and is_odd:
                pltpu.sync_copy(q_refs[1], qs.at[pl.ds(0, ROWS + META)])
            else:
                qs[: ROWS + META] = q_refs[0][...]
            os[...] = jnp.zeros_like(os)
            ls[...] = jnp.zeros_like(ls)
            firsts = qs[ROWS : ROWS + META].astype(F32)
            for g in range(GROUPS):
                starts[g] = jnp.max(firsts[g : g + 1]).astype(I32)
            if kind == "own":
                eye = iota((128, 128), 0) == iota((128, 128), 1)
                for b in range(BLOCKS):
                    picked = jnp.where(eye, pos_ref[b : b + 1], F32(0))
                    reach = jnp.sum(picked, axis=1, keepdims=True)
                    ps[b * 128 : (b + 1) * 128] = jnp.broadcast_to(reach, (128, 128))

        units = []
        for i in range(STEP):
            start = pl.multiple_of(starts[step * STEP + i] * 16, 16)
            parts = shard_parts(i, is_odd)
            for c in range(MOST_GROUP // CHUNK):
                units.append((pl.ds(pl.multiple_of(start + c * CHUNK, 16), CHUNK), parts))
        scored = []
        for rows, parts in units:
            q = qs[rows, :]
            scores = []
            for k, _, _, causal in parts:
                s = dot_t(q, k)
                if causal:
                    reach = ps[rows, :][:, :1]
                    s = jnp.where(iota(s.shape, 1).astype(F32) <= reach, s, F32(LOW))
                scores.append(s)
            scored.append(scores)
        tops = []
        for (rows, parts), scores in zip(units, scored):
            peaks = []
            for s, (_, _, bias, _) in zip(scores, parts):
                peak = jnp.max(s, axis=1, keepdims=True)
                peaks.append(peak if bias is None else peak + bias)
            tops.append(functools.reduce(jnp.maximum, peaks))
        results = []
        for (rows, parts), scores, top in zip(units, scored, tops):
            both = None
            for s, (_, v, bias, _) in zip(scores, parts):
                base = top if bias is None else top - bias
                weight = jnp.exp2((s - base) * F32(SCALE)).astype(BF16)
                product = dot(weight, jnp.concatenate([v, jnp.ones_like(v)], axis=1))
                both = product if both is None else both + product
            results.append(both)
        for (rows, parts), both, top in zip(units, results, tops):
            total = both[:, 128:]
            os[rows, :] = (both[:, :128] / total).astype(BF16)
            ls[rows, :] = top * F32(SCALE) + jnp.log2(total)

        @pl.when(step == GROUPS // STEP - 1)
        def _():
            out_ref[:ROWS] = os[:ROWS]
            eye = iota((128, 128), 0) == iota((128, 128), 1)
            tail[...] = jnp.zeros_like(tail)
            for b in range(BLOCKS):
                square = ls[b * 128 : (b + 1) * 128]
                line = jnp.sum(jnp.where(eye, square, F32(0)), axis=0, keepdims=True)
                high = line.astype(BF16).astype(F32)
                middle = (line - high).astype(BF16).astype(F32)
                tail[b : b + 1] = high
                tail[BLOCKS + b : BLOCKS + b + 1] = middle
                tail[2 * BLOCKS + b : 2 * BLOCKS + b + 1] = line - high - middle
            out_ref[ROWS:] = tail[...].astype(BF16)

    if kind == "own":
        work(False)
    else:
        pl.when(odd == 0)(lambda: work(False))
        pl.when(odd == 1)(lambda: work(True))


def attend(kind, flags, packed, kvs, pos=None):
    kv_spec = pl.BlockSpec((2, STEP, 512, 128), lambda g: (0, g, 0, 0))

    def whole(rows):
        return pl.BlockSpec((rows, 128), lambda g: (0, 0))

    in_specs = [pl.BlockSpec(memory_space=pltpu.SMEM)]
    in_specs += [whole(ROWS + META)] + [pl.BlockSpec(memory_space=pltpu.HBM)] * (len(packed) - 1)
    in_specs += [kv_spec] * len(kvs)
    args = [flags, *packed, *kvs]
    scratch = [pltpu.VMEM((SPAN, 128), BF16), pltpu.VMEM((SPAN, 128), BF16), pltpu.VMEM((SPAN, 128), F32)]
    scratch += [pltpu.VMEM((TAIL, 128), F32), pltpu.SMEM((GROUPS,), I32)]
    if kind == "own":
        in_specs.append(whole(LINES))
        args.append(pos)
        scratch.append(pltpu.VMEM((SPAN, 128), F32))
    return pl.pallas_call(
        functools.partial(attend_kernel, kind),
        grid=(GROUPS // STEP,),
        in_specs=in_specs,
        out_specs=whole(ROWS + TAIL),
        out_shape=jax.ShapeDtypeStruct((ROWS + TAIL, 128), BF16),
        scratch_shapes=scratch,
        compiler_params=pltpu.CompilerParams(
            dimension_semantics=("arbitrary",), vmem_limit_bytes=LIMIT
        ),
        cost_estimate=SMALL,
        name="attend_" + kind,
    )(*args)


def lines_of(tail):
    tail = tail.astype(F32)
    return tail[:BLOCKS] + tail[BLOCKS : 2 * BLOCKS] + tail[2 * BLOCKS : 3 * BLOCKS]


def mix(lines, b, on):
    first, second = lines[0][b : b + 1], jnp.where(on, lines[1][b : b + 1], F32(LOW))
    top = jnp.maximum(first, second)
    total = jnp.exp2(first - top) + jnp.exp2(second - top)
    eye = iota((128, 128), 0) == iota((128, 128), 1)
    share = jnp.exp2(second - top) / total
    column = jnp.sum(jnp.where(eye, share, F32(0)), axis=1, keepdims=True)
    return column, top + jnp.log2(total)


def mix_kernel(flags, own_ref, back_ref, here_ref, sum_ref, lines_ref):
    odd, chip = flags[0], flags[1]

    def run(other, on):
        lines = lines_of(own_ref[ROWS:]), lines_of(other[ROWS:])
        lines_ref[...] = jnp.zeros_like(lines_ref)
        for b in range(BLOCKS):
            rows = slice(b * 128, (b + 1) * 128)
            share, line = mix(lines, b, on)
            own = own_ref[rows].astype(F32)
            sum_ref[rows] = (own + share * (other[rows].astype(F32) - own)).astype(BF16)
            lines_ref[b : b + 1] = line

    pl.when(odd == 0)(lambda: run(back_ref, chip >= 1))
    pl.when(odd == 1)(lambda: run(here_ref, odd == 1))


def mix_early(flags, own, back, here):
    return pl.pallas_call(
        mix_kernel,
        in_specs=[pl.BlockSpec(memory_space=pltpu.SMEM)] + [pl.BlockSpec(memory_space=pltpu.VMEM)] * 3,
        out_shape=[jax.ShapeDtypeStruct((ROWS, 128), BF16), jax.ShapeDtypeStruct((LINES, 128), F32)],
        compiler_params=pltpu.CompilerParams(vmem_limit_bytes=24 * 2**20),
        cost_estimate=SMALL,
        name="mix_early",
    )(flags, own, back, here)


def finish_kernel(flags, sum_ref, lines_ref, near_ref, far_ref, slots_ref, out_ref, merged):
    odd, chip = flags[0], flags[1]

    def merge(late_ref, on):
        lines = lines_ref[:BLOCKS], lines_of(late_ref[ROWS:])
        for b in range(BLOCKS):
            rows = slice(b * 128, (b + 1) * 128)
            share, _ = mix(lines, b, on)
            early = sum_ref[rows].astype(F32)
            merged[rows] = (early + share * (late_ref[rows].astype(F32) - early)).astype(BF16)

    pl.when(odd == 1)(lambda: merge(near_ref, chip >= 1))
    pl.when(odd == 0)(lambda: merge(far_ref, chip >= 2))
    entries = out_ref.shape[0]
    for e in range(entries // 256):
        rows = slice(e * 256, (e + 1) * 256)
        place = one_hot(iota((256, ROWS), 1) == slots_ref[rows])
        out_ref[rows] = dot(place, merged[...]).astype(BF16)


def finish(flags, early, lines, near, far, slots_column):
    entries = slots_column.shape[0]
    return pl.pallas_call(
        finish_kernel,
        in_specs=[pl.BlockSpec(memory_space=pltpu.SMEM)] + [pl.BlockSpec(memory_space=pltpu.VMEM)] * 5,
        out_shape=jax.ShapeDtypeStruct((entries, 128), BF16),
        scratch_shapes=[pltpu.VMEM((ROWS, 128), BF16)],
        compiler_params=pltpu.CompilerParams(vmem_limit_bytes=24 * 2**20),
        cost_estimate=SMALL,
        name="finish",
    )(flags, early, lines, near, far, slots_column)


def moved(block, distance):
    devices = range(lax.axis_size("seq"))
    pairs = [(i, i + distance(i)) for i in devices if distance(i) and i + distance(i) in devices]
    return lax.ppermute(block, "seq", pairs)


def shards(queries, keys, values, routes):
    tokens, routed, width = queries.shape
    devices = range(lax.axis_size("seq"))
    device = lax.axis_index("seq").astype(I32)
    flags = jnp.stack([device % 2, device // 2])

    def after(x, *others):
        return lax.optimization_barrier((x, *others))[0]

    kv = jnp.stack([keys.transpose(1, 0, 2), values.transpose(1, 0, 2)])
    kv_forward = moved(kv, lambda i: 2 if i % 2 else 0)
    packed, pos, slots = sort_queries(after(routes.T, kv), queries.transpose(1, 0, 2).reshape(-1, width))
    column = slots.T.reshape(-1, 1)
    near_q = moved(packed, lambda i: -2)
    own = attend("own", flags, [packed], [kv], pos)
    kv_sibling = moved(kv, lambda i: -1 if i % 2 else 1)
    far_q = moved(after(packed, own, column), lambda i: 0 if i % 2 else -4)
    near_q = after(near_q, own)
    near_out = attend("near", flags, [near_q], [kv, kv_sibling, kv_forward])
    near_back = moved(near_out, lambda i: 2)
    far_q = after(far_q, near_out)
    far_out = attend("far", flags, [far_q, packed], [kv, kv_sibling])
    far_back = moved(far_out, lambda i: 0 if i % 2 else 4)
    early_sum, early_lines = mix_early(flags, own, near_back, far_out)
    out = finish(flags, early_sum, early_lines, near_back, after(far_back, early_sum), column)
    return out.reshape(tokens, routed, width)


def solution(mesh):
    placed = (P("seq", None, None), P("seq", None, None), P("seq", None, None), P("seq", None))
    return jax.shard_map(
        shards, mesh=mesh, in_specs=placed, out_specs=P("seq", None, None), check_vma=False
    )
```

time: 88.2 us -> 86.2 us (0.977)
  the two profiles are of different devices: /device:TPU:57 before, /device:TPU:120 now
where the time goes in v2:
time: 86.2 us; the launch traced here: 85.8 us
  waiting for transfers between devices  29.6 us (34%)
  starting transfers between devices  27.9 us (32%)
  Pallas kernels  24.2 us (28%)
  local copies, waits for them, and re-layouts  3.66 us (4%)
    ppermute x6, waiting for transfers between devices, moved(): return lax.ppermute(block, 'seq', pairs)  29.6 us
    ppermute x6, starting transfers between devices, moved(): return lax.ppermute(block, 'seq', pairs)  27.9 us
    pallas_call x3, Pallas kernels, attend(): pl.pallas_call(functools.partial(attend_kernel, kind), grid=(GROUPS // ST...  14.9 us
    pallas_call x1, Pallas kernels, finish(): pl.pallas_call(finish_kernel, in_specs=[pl.BlockSpec(memory_space=pltpu.S...  4.81 us
    pallas_call x1, Pallas kernels, sort_queries(): pl.pallas_call(sort_kernel, out_shape=[jax.ShapeDtypeStruct((ROWS + META,...  3.04 us
    another operation x1, local copies, waits for them, and re-layouts, shards(): kv = jnp.stack([keys.transpose(1, 0, 2), values.transpose(1, 0, 2)])  1.92 us
  transfers between devices with their start and end apart: 6, of which 3 were waited for; matrix products, arithmetic and copies ran while one was open for 1% of the time, Pallas kernels for 23%

profile of v2, /device:TPU:120, one launch (start us, length us, event | category | flops | bytes accessed | tf_op | source)
XLA Modules:
  0.0 85.8 jit_solution(10203934827244178057)
XLA Ops:
  0.0 1.9 %copy_bitcast_fusion = (bf16[1,8,512,128]{3,2,1,0:T(8,128)(2,1)S(1)}, bf16[1,8,512,128]{3,2,1,0:T(8,128)(2,1)S(1)}) fusion(bf16[512,8,128]{2,1,0:T(8,128)(2,1)} %param.6, bf16[512,8,128]{2,1,0:T(8,128)(2,1)} %param.5), kind=kLoop, calls=%fused_computation.1 | loop fusion | bytes 4194304 | tf_op jit(solution)/shard_map/stack | solution.py:318
  1.9 0.0 copy-start.3
  1.9 0.0 copy-start.2
  2.0 0.2 pad_maximum_fusion.refs_1_.refs_2_
  2.2 1.9 %collective-permute-start.1 = (bf16[2,8,512,128]{3,2,1,0:T(8,128)(2,1)S(1)}, bf16[2,8,512,128]{3,2,1,0:T(8,128)(2,1)}, u32[]{:S(2)}, u32[]{:S(2)}) collective-permute-start(bf16[2,8,512,128]{3,2,1,0:T(8,128)(2,1)S(1)} %pad_maximum_fusion.refs_1_.refs_2_), channel_id=1, source_target_pairs={{0,1},{1,0},{2,3},{3,2},{4,5},{5,4},{6,7},{7,6},{8,9},{9,8},{10,11... | collective-permute-start | bytes 6291464 | tf_op jit(solution)/shard_map/ppermute | solution.py:306
  4.1 2.0 %collective-permute-start.2 = (bf16[2,8,512,128]{3,2,1,0:T(8,128)(2,1)S(1)}, bf16[2,8,512,128]{3,2,1,0:T(8,128)(2,1)}, u32[]{:S(2)}, u32[]{:S(2)}) collective-permute-start(bf16[2,8,512,128]{3,2,1,0:T(8,128)(2,1)S(1)} %pad_maximum_fusion.refs_1_.refs_2_), channel_id=1, source_target_pairs={{1,3},{3,5},{5,7},{7,9},{9,11},{11,13},{13,15},{15,17},{17,19},{19... | collective-permute-start | bytes 6291464 | tf_op jit(solution)/shard_map/ppermute | solution.py:306
  6.1 0.0 copy-done.3
  6.1 0.1 copy.11
  6.1 0.0 copy-done.2
  6.2 3.0 %sort_queries.1 = (bf16[2192,128]{1,0:T(8,128)(2,1)S(1)}, f32[24,128]{1,0:T(8,128)S(1)}, s32[8,256]{1,0:T(8,128)S(1)}) custom-call(s32[8,256]{1,0:T(8,128)S(1)} %bitcast.16, bf16[2048,128]{1,0:T(8,128)(2,1)S(1)} %bitcast.15), custom_call_target="tpu_custom_call" | custom-call | flops 1000 | bytes 1000 | tf_op jit(solution)/shard_map/sort_queries/pallas_call | solution.py:77
  9.2 0.0 copy-start
  9.2 1.9 %collective-permute-start = (bf16[2192,128]{1,0:T(8,128)(2,1)S(1)}, bf16[2192,128]{1,0:T(8,128)(2,1)}, u32[]{:S(2)}, u32[]{:S(2)}) collective-permute-start(bf16[2192,128]{1,0:T(8,128)(2,1)S(1)} %get-tuple-element.20.refs_0_.refs_1_), channel_id=1, source_target_pairs={{2,0},{3,1},{4,2},{5,3},{6,4},{7,5},{8,6},{9,7},{10,8},{11,9},{12,... | collective-permute-start | bytes 1683464 | tf_op jit(solution)/shard_map/ppermute | solution.py:306
  11.2 0.1 pad_add_fusion.flags
  11.2 3.6 %attend_own.1.own_ref = bf16[2240,128]{1,0:T(8,128)(2,1)S(1)} custom-call(s32[2]{0:T(128)S(1)} %pad_add_fusion.flags, bf16[2192,128]{1,0:T(8,128)(2,1)S(1)} %get-tuple-element.20.refs_0_.refs_1_, bf16[2,8,512,128]{3,2,1,0:T(8,128)(2,1)S(1)} %pad_maximum_fusion.refs_1_.refs_2_, f32[24,128]{1,0:T(8,128)S(1)} %get-tuple-element.17.refs_2_), custom_call_target="tpu_custom_call" | custom-call | flops 1000 | bytes 1000 | tf_op jit(solution)/shard_map/attend_own/pallas_call | solution.py:212
  14.8 0.1 copy.12
  15.0 0.1 reshape.10
  15.1 13.6 %collective-permute-start.4 = (bf16[2192,128]{1,0:T(8,128)(2,1)S(1)}, bf16[2192,128]{1,0:T(8,128)(2,1)S(1)}, u32[]{:S(2)}, u32[]{:S(2)}) collective-permute-start(bf16[2192,128]{1,0:T(8,128)(2,1)S(1)} %get-tuple-element.20.refs_0_.refs_1_), channel_id=1, source_target_pairs={{4,0},{6,2},{8,4},{10,6},{12,8},{14,10},{16,12},{18,14},{20,16},{2... | collective-permute-start | bytes 1683464 | tf_op jit(solution)/shard_map/ppermute | solution.py:306
  28.7 0.0 collective-permute-done.refs_0_
  28.7 0.0 collective-permute-done.1.refs_2_.refs_3_
  28.7 0.0 collective-permute-done.2.refs_3_
  28.7 6.3 %attend_near.1 = bf16[2240,128]{1,0:T(8,128)(2,1)} custom-call(s32[2]{0:T(128)S(1)} %pad_add_fusion.flags, bf16[2192,128]{1,0:T(8,128)(2,1)} %collective-permute-done.refs_0_, bf16[2,8,512,128]{3,2,1,0:T(8,128)(2,1)S(1)} %pad_maximum_fusion.refs_1_.refs_2_, bf16[2,8,512,128]{3,2,1,0:T(8,128)(2,1)} %collective-permute-done.1.refs_2_.refs_3_, ...), custom_call_target="tpu_custom_call" | custom-call | flops 1000 | bytes 1000 | tf_op jit(solution)/shard_map/attend_near/pallas_call | solution.py:212
  35.0 0.0 copy-done
  35.0 3.6 %collective-permute-start.3 = (bf16[2240,128]{1,0:T(8,128)(2,1)}, bf16[2240,128]{1,0:T(8,128)(2,1)}, u32[]{:S(2)}, u32[]{:S(2)}) collective-permute-start(bf16[2240,128]{1,0:T(8,128)(2,1)} %attend_near.1), channel_id=1, source_target_pairs={{0,2},{1,3},{2,4},{3,5},{4,6},{5,7},{6,8},{7,9},{8,10},{9,11},{10,... | collective-permute-start | bytes 1720328 | tf_op jit(solution)/shard_map/ppermute | solution.py:306
  38.6 0.8 collective-permute-done.4.refs_0_
  39.3 0.0 copy-start.1
  39.3 1.1 %copy-done.1 = bf16[2192,128]{1,0:T(8,128)(2,1)S(1)} copy-done((bf16[2192,128]{1,0:T(8,128)(2,1)S(1)}, bf16[2192,128]{1,0:T(8,128)(2,1)}, u32[]{:S(2)}) %copy-start.1) | copy-done | bytes 561176
  40.4 5.0 %attend_far.1.here_ref = bf16[2240,128]{1,0:T(8,128)(2,1)S(1)} custom-call(s32[2]{0:T(128)S(1)} %pad_add_fusion.flags, bf16[2192,128]{1,0:T(8,128)(2,1)S(1)} %collective-permute-done.4.refs_0_, bf16[2192,128]{1,0:T(8,128)(2,1)S(1)} %copy-done.1, bf16[2,8,512,128]{3,2,1,0:T(8,128)(2,1)S(1)} %pad_maximum_fusion.refs_1_.refs_2_, ...), custom_call_target="tpu_custom_call" | custom-call | flops 1000 | bytes 1000 | tf_op jit(solution)/shard_map/attend_far/pallas_call | solution.py:212
  45.4 4.9 %collective-permute-start.5 = (bf16[2240,128]{1,0:T(8,128)(2,1)S(1)}, bf16[2240,128]{1,0:T(8,128)(2,1)S(1)}, u32[]{:S(2)}, u32[]{:S(2)}) collective-permute-start(bf16[2240,128]{1,0:T(8,128)(2,1)S(1)} %attend_far.1.here_ref), channel_id=1, source_target_pairs={{0,4},{2,6},{4,8},{6,10},{8,12},{10,14},{12,16},{14,18},{16,20},{1... | collective-permute-start | bytes 1720328 | tf_op jit(solution)/shard_map/ppermute | solution.py:306
  50.3 0.4 copy.13.slots_ref
  50.7 7.5 %collective-permute-done.3.back_ref.near_ref = bf16[2240,128]{1,0:T(8,128)(2,1)} collective-permute-done((bf16[2240,128]{1,0:T(8,128)(2,1)}, bf16[2240,128]{1,0:T(8,128)(2,1)}, u32[]{:S(2)}, u32[]{:S(2)}) %collective-permute-start.3) | collective-permute-done | bytes 573472 | tf_op jit(solution)/shard_map/ppermute | solution.py:306
  58.2 1.5 %mix_early.1 = (bf16[2176,128]{1,0:T(8,128)(2,1)S(1)}, f32[24,128]{1,0:T(8,128)S(1)}) custom-call(s32[2]{0:T(128)S(1)} %pad_add_fusion.flags, bf16[2240,128]{1,0:T(8,128)(2,1)S(1)} %attend_own.1.own_ref, bf16[2240,128]{1,0:T(8,128)(2,1)} %collective-permute-done.3.back_ref.near_ref, bf16[2240,128]{1,0:T(8,128)(2,1)S(1)} %attend_far.1.here_ref), custom_call_target="tpu_custom_call" | custom-call | flops 1000 | bytes 1000 | tf_op jit(solution)/shard_map/mix_early/pallas_call | solution.py:260
  59.7 21.3 %collective-permute-done.5.far_ref = bf16[2240,128]{1,0:T(8,128)(2,1)S(1)} collective-permute-done((bf16[2240,128]{1,0:T(8,128)(2,1)S(1)}, bf16[2240,128]{1,0:T(8,128)(2,1)S(1)}, u32[]{:S(2)}, u32[]{:S(2)}) %collective-permute-start.5) | collective-permute-done | bytes 573472 | tf_op jit(solution)/shard_map/ppermute | solution.py:306
  81.0 4.8 %finish.1 = bf16[2048,128]{1,0:T(8,128)(2,1)} custom-call(s32[2]{0:T(128)S(1)} %pad_add_fusion.flags, bf16[2176,128]{1,0:T(8,128)(2,1)S(1)} %get-tuple-element.22.sum_ref, f32[24,128]{1,0:T(8,128)S(1)} %get-tuple-element.23.lines_ref, bf16[2240,128]{1,0:T(8,128)(2,1)} %collective-permute-done.3.back_ref.near_ref, ...), custom_call_target="tpu_custom_call" | custom-call | flops 1000 | bytes 1000 | tf_op jit(solution)/shard_map/finish/pallas_call | solution.py:292
Async XLA Ops:
  1.9 4.1 %copy-start.3 = (bf16[256,8,128]{2,1,0:T(8,128)(2,1)S(1)}, bf16[256,8,128]{2,1,0:T(8,128)(2,1)}, u32[]{:S(2)}) copy-start(bf16[256,8,128]{2,1,0:T(8,128)(2,1)} %param.4) | copy-start | bytes 1572868
  1.9 4.2 %copy-start.2 = (s32[256,8]{0,1:T(8,128)S(1)}, s32[256,8]{0,1:T(8,128)}, u32[]{:S(2)}) copy-start(s32[256,8]{0,1:T(8,128)} %param.7) | copy-start | bytes 24580
  2.2 26.5 %collective-permute-start.1 = (bf16[2,8,512,128]{3,2,1,0:T(8,128)(2,1)S(1)}, bf16[2,8,512,128]{3,2,1,0:T(8,128)(2,1)}, u32[]{:S(2)}, u32[]{:S(2)}) collective-permute-start(bf16[2,8,512,128]{3,2,1,0:T(8,128)(2,1)S(1)} %pad_maximum_fusion.refs_1_.refs_2_), channel_id=1, source_target_pairs={{0,1},{1,0},{2,3},{3,2},{4,5},{5,4},{6,7},{7,6},{8,9},{9,8},{10,11... | collective-permute-start | bytes 6291464 | tf_op jit(solution)/shard_map/ppermute | solution.py:306
  4.1 24.6 %collective-permute-start.2 = (bf16[2,8,512,128]{3,2,1,0:T(8,128)(2,1)S(1)}, bf16[2,8,512,128]{3,2,1,0:T(8,128)(2,1)}, u32[]{:S(2)}, u32[]{:S(2)}) collective-permute-start(bf16[2,8,512,128]{3,2,1,0:T(8,128)(2,1)S(1)} %pad_maximum_fusion.refs_1_.refs_2_), channel_id=1, source_target_pairs={{1,3},{3,5},{5,7},{7,9},{9,11},{11,13},{13,15},{15,17},{17,19},{19... | collective-permute-start | bytes 6291464 | tf_op jit(solution)/shard_map/ppermute | solution.py:306
  9.2 25.8 %copy-start = (bf16[2192,128]{1,0:T(8,128)(2,1)}, bf16[2192,128]{1,0:T(8,128)(2,1)S(1)}, u32[]{:S(2)}) copy-start(bf16[2192,128]{1,0:T(8,128)(2,1)S(1)} %get-tuple-element.20.refs_0_.refs_1_) | copy-start | bytes 1683460
  9.2 19.5 %collective-permute-start = (bf16[2192,128]{1,0:T(8,128)(2,1)S(1)}, bf16[2192,128]{1,0:T(8,128)(2,1)}, u32[]{:S(2)}, u32[]{:S(2)}) collective-permute-start(bf16[2192,128]{1,0:T(8,128)(2,1)S(1)} %get-tuple-element.20.refs_0_.refs_1_), channel_id=1, source_target_pairs={{2,0},{3,1},{4,2},{5,3},{6,4},{7,5},{8,6},{9,7},{10,8},{11,9},{12,... | collective-permute-start | bytes 1683464 | tf_op jit(solution)/shard_map/ppermute | solution.py:306
  15.1 24.2 %collective-permute-start.4 = (bf16[2192,128]{1,0:T(8,128)(2,1)S(1)}, bf16[2192,128]{1,0:T(8,128)(2,1)S(1)}, u32[]{:S(2)}, u32[]{:S(2)}) collective-permute-start(bf16[2192,128]{1,0:T(8,128)(2,1)S(1)} %get-tuple-element.20.refs_0_.refs_1_), channel_id=1, source_target_pairs={{4,0},{6,2},{8,4},{10,6},{12,8},{14,10},{16,12},{18,14},{20,16},{2... | collective-permute-start | bytes 1683464 | tf_op jit(solution)/shard_map/ppermute | solution.py:306
  35.0 23.2 %collective-permute-start.3 = (bf16[2240,128]{1,0:T(8,128)(2,1)}, bf16[2240,128]{1,0:T(8,128)(2,1)}, u32[]{:S(2)}, u32[]{:S(2)}) collective-permute-start(bf16[2240,128]{1,0:T(8,128)(2,1)} %attend_near.1), channel_id=1, source_target_pairs={{0,2},{1,3},{2,4},{3,5},{4,6},{5,7},{6,8},{7,9},{8,10},{9,11},{10,... | collective-permute-start | bytes 1720328 | tf_op jit(solution)/shard_map/ppermute | solution.py:306
  39.3 1.1 %copy-start.1 = (bf16[2192,128]{1,0:T(8,128)(2,1)S(1)}, bf16[2192,128]{1,0:T(8,128)(2,1)}, u32[]{:S(2)}) copy-start(bf16[2192,128]{1,0:T(8,128)(2,1)} %copy-done) | copy-start | bytes 1683460
  45.4 35.6 %collective-permute-start.5 = (bf16[2240,128]{1,0:T(8,128)(2,1)S(1)}, bf16[2240,128]{1,0:T(8,128)(2,1)S(1)}, u32[]{:S(2)}, u32[]{:S(2)}) collective-permute-start(bf16[2240,128]{1,0:T(8,128)(2,1)S(1)} %attend_far.1.here_ref), channel_id=1, source_target_pairs={{0,4},{2,6},{4,8},{6,10},{8,12},{10,14},{12,16},{14,18},{16,20},{1... | collective-permute-start | bytes 1720328 | tf_op jit(solution)/shard_map/ppermute | solution.py:306

commit v3 on v2

--- a/solution.py
+++ b/solution.py
@@ -105,10 +105,10 @@
                 (kv[0][0, i, :256], kv[0][1, i, :256], None, False),
                 (kv[0][0, i, 256:], kv[0][1, i, 256:], None, True),
             ]
-        sibling = (kv[1][0, i], kv[1][1, i], None, False)
+        parts = [(kv[0][0, i], kv[0][1, i], None, False)]
         if kind == "far" and is_odd:
-            return [sibling]
-        parts = [(kv[0][0, i], kv[0][1, i], None, False), sibling]
+            return parts
+        parts.append((kv[1][0, i], kv[1][1, i], None, False))
         if is_odd:
             flag = jnp.where(chip >= 1, F32(0), F32(LOW))
             parts.append((kv[2][0, i], kv[2][1, i], flag, False))
@@ -195,13 +195,16 @@
 
 def attend(kind, flags, packed, kvs, pos=None):
     kv_spec = pl.BlockSpec((2, STEP, 512, 128), lambda g: (0, g, 0, 0))
+    first = pl.BlockSpec((None, 2, STEP, 512, 128), lambda g: (0, 0, g, 0, 0))
+    second = pl.BlockSpec((None, 2, STEP, 512, 128), lambda g: (1, 0, g, 0, 0))
+    kv_specs = {"own": [kv_spec], "near": [first, second, kv_spec], "far": [first, second]}[kind]
 
     def whole(rows):
         return pl.BlockSpec((rows, 128), lambda g: (0, 0))
 
     in_specs = [pl.BlockSpec(memory_space=pltpu.SMEM)]
     in_specs += [whole(ROWS + META)] + [pl.BlockSpec(memory_space=pltpu.HBM)] * (len(packed) - 1)
-    in_specs += [kv_spec] * len(kvs)
+    in_specs += kv_specs
     args = [flags, *packed, *kvs]
     scratch = [pltpu.VMEM((SPAN, 128), BF16), pltpu.VMEM((SPAN, 128), BF16), pltpu.VMEM((SPAN, 128), F32)]
     scratch += [pltpu.VMEM((TAIL, 128), F32), pltpu.SMEM((GROUPS,), I32)]
@@ -321,13 +324,14 @@
     column = slots.T.reshape(-1, 1)
     near_q = moved(packed, lambda i: -2)
     own = attend("own", flags, [packed], [kv], pos)
-    kv_sibling = moved(kv, lambda i: -1 if i % 2 else 1)
+    pairs = [[i, i + 1] for i in range(0, lax.axis_size("seq"), 2)]
+    chip_kv = lax.all_gather(kv, "seq", axis_index_groups=pairs)
     far_q = moved(after(packed, own, column), lambda i: 0 if i % 2 else -4)
     near_q = after(near_q, own)
-    near_out = attend("near", flags, [near_q], [kv, kv_sibling, kv_forward])
+    near_out = attend("near", flags, [near_q], [chip_kv, chip_kv, kv_forward])
     near_back = moved(near_out, lambda i: 2)
     far_q = after(far_q, near_out)
-    far_out = attend("far", flags, [far_q, packed], [kv, kv_sibling])
+    far_out = attend("far", flags, [far_q, packed], [chip_kv, chip_kv])
     far_back = moved(far_out, lambda i: 0 if i % 2 else 4)
     early_sum, early_lines = mix_early(flags, own, near_back, far_out)
     out = finish(flags, early_sum, early_lines, near_back, after(far_back, early_sum), column)

time: 86.2 us -> 101 us (1.17)
  the two profiles are of different devices: /device:TPU:120 before, /device:TPU:112 now
where the time goes in v3:
time: 101 us
  waiting for transfers between devices  28 us (28%)
  starting transfers between devices  26.8 us (27%)
  Pallas kernels  24.5 us (24%)
  between operations  13.6 us (13%)
  local copies, waits for them, and re-layouts  6.35 us (6%)
  other arithmetic  1.6 us (2%)
    ppermute x5, waiting for transfers between devices, moved(): return lax.ppermute(block, 'seq', pairs)  27.9 us
    ppermute x5, starting transfers between devices, moved(): return lax.ppermute(block, 'seq', pairs)  26.8 us
    pallas_call x3, Pallas kernels, attend(): pl.pallas_call(functools.partial(attend_kernel, kind), grid=(GROUPS // ST...  14.9 us
    pallas_call x1, Pallas kernels, finish(): pl.pallas_call(finish_kernel, in_specs=[pl.BlockSpec(memory_space=pltpu.S...  4.8 us
    pallas_call x1, Pallas kernels, sort_queries(): pl.pallas_call(sort_kernel, out_shape=[jax.ShapeDtypeStruct((ROWS + META,...  3.88 us
    unnamed x8, local copies, waits for them, and re-layouts  3.76 us
  transfers between devices with their start and end apart: 6, of which 2 were waited for; matrix products, arithmetic and copies ran while one was open for 1% of the time, Pallas kernels for 20%

profile of v3, /device:TPU:112, one launch (start us, length us, event | category | flops | bytes accessed | tf_op | source)
XLA Modules:
  0.0 100.8 jit_solution(17834334857547510722)
XLA Ops:
  6.5 0.0 all-gather.3.cloned.1.call-start
  6.5 1.9 %copy_bitcast_fusion = (bf16[1,8,512,128]{3,2,1,0:T(8,128)(2,1)S(1)}, bf16[1,8,512,128]{3,2,1,0:T(8,128)(2,1)S(1)}) fusion(bf16[512,8,128]{2,1,0:T(8,128)(2,1)} %param.6, bf16[512,8,128]{2,1,0:T(8,128)(2,1)} %param.5), kind=kLoop, calls=%fused_computation.1 | loop fusion | bytes 4194304 | tf_op jit(solution)/shard_map/stack | solution.py:321
  8.5 0.0 copy-start.3
  8.5 1.5 %pad_maximum_fusion.refs_1_ = bf16[2,8,512,128]{3,2,1,0:T(8,128)(2,1)} fusion(bf16[1,8,512,128]{3,2,1,0:T(8,128)(2,1)S(1)} %get-tuple-element.25, bf16[1,8,512,128]{3,2,1,0:T(8,128)(2,1)S(1)} %get-tuple-element.26), kind=kLoop, calls=%fused_computation | loop fusion | flops 1048576 | bytes 4194304 | tf_op jit(solution)/shard_map/stack | solution.py:321
  10.0 0.0 copy-start.1
  10.0 0.0 copy-start.2
  10.0 0.0 all-gather.3.cloned.1.call-update
  10.0 1.6 %copy-done.1 = bf16[2,8,512,128]{3,2,1,0:T(8,128)(2,1)S(1)} copy-done((bf16[2,8,512,128]{3,2,1,0:T(8,128)(2,1)S(1)}, bf16[2,8,512,128]{3,2,1,0:T(8,128)(2,1)}, u32[]{:S(2)}) %copy-start.1) | copy-done | bytes 2097176
  11.6 2.0 %collective-permute-start.1 = (bf16[2,8,512,128]{3,2,1,0:T(8,128)(2,1)S(1)}, bf16[2,8,512,128]{3,2,1,0:T(8,128)(2,1)}, u32[]{:S(2)}, u32[]{:S(2)}) collective-permute-start(bf16[2,8,512,128]{3,2,1,0:T(8,128)(2,1)S(1)} %copy-done.1), channel_id=1, source_target_pairs={{1,3},{3,5},{5,7},{7,9},{9,11},{11,13},{13,15},{15,17},{17,19},{19... | collective-permute-start | bytes 6291464 | tf_op jit(solution)/shard_map/ppermute | solution.py:309
  13.6 0.0 copy-done.3
  13.6 0.1 copy.16
  13.7 0.0 copy-done.2
  13.7 3.9 %sort_queries.1 = (bf16[2192,128]{1,0:T(8,128)(2,1)}, f32[24,128]{1,0:T(8,128)S(1)}, s32[8,256]{1,0:T(8,128)S(1)}) custom-call(s32[8,256]{1,0:T(8,128)S(1)} %bitcast.21, bf16[2048,128]{1,0:T(8,128)(2,1)S(1)} %bitcast.20), custom_call_target="tpu_custom_call" | custom-call | flops 1000 | bytes 1000 | tf_op jit(solution)/shard_map/sort_queries/pallas_call | solution.py:77
  17.6 1.9 %collective-permute-start = (bf16[2192,128]{1,0:T(8,128)(2,1)}, bf16[2192,128]{1,0:T(8,128)(2,1)S(1)}, u32[]{:S(2)}, u32[]{:S(2)}) collective-permute-start(bf16[2192,128]{1,0:T(8,128)(2,1)} %get-tuple-element.20.refs_0_.refs_1_), channel_id=1, source_target_pairs={{2,0},{3,1},{4,2},{5,3},{6,4},{7,5},{8,6},{9,7},{10,8},{11,9},{12,... | collective-permute-start | bytes 1683464 | tf_op jit(solution)/shard_map/ppermute | solution.py:309
  19.5 0.1 pad_add_fusion.flags
  19.6 4.1 %attend_own.1.own_ref = bf16[2240,128]{1,0:T(8,128)(2,1)S(1)} custom-call(s32[2]{0:T(128)S(1)} %pad_add_fusion.flags, bf16[2192,128]{1,0:T(8,128)(2,1)} %get-tuple-element.20.refs_0_.refs_1_, bf16[2,8,512,128]{3,2,1,0:T(8,128)(2,1)S(1)} %copy-done.1, f32[24,128]{1,0:T(8,128)S(1)} %get-tuple-element.17.refs_2_), custom_call_target="tpu_custom_call" | custom-call | flops 1000 | bytes 1000 | tf_op jit(solution)/shard_map/attend_own/pallas_call | solution.py:215
  23.7 0.1 copy.17
  23.8 0.1 reshape.10
  24.0 13.6 %collective-permute-start.3 = (bf16[2192,128]{1,0:T(8,128)(2,1)}, bf16[2192,128]{1,0:T(8,128)(2,1)}, u32[]{:S(2)}, u32[]{:S(2)}) collective-permute-start(bf16[2192,128]{1,0:T(8,128)(2,1)} %get-tuple-element.20.refs_0_.refs_1_), channel_id=1, source_target_pairs={{4,0},{6,2},{8,4},{10,6},{12,8},{14,10},{16,12},{18,14},{20,16},{2... | collective-permute-start | bytes 1683464 | tf_op jit(solution)/shard_map/ppermute | solution.py:309
  37.5 0.0 collective-permute-done.refs_0_
  37.5 0.0 collective-permute-done.1.refs_3_
  37.6 0.0 all-gather.3.cloned.1.call-done
  37.6 0.0 copy-start
  37.6 2.2 %copy-done = bf16[4,8,512,128]{3,2,1,0:T(8,128)(2,1)S(1)} copy-done((bf16[4,8,512,128]{3,2,1,0:T(8,128)(2,1)S(1)}, bf16[4,8,512,128]{3,2,1,0:T(8,128)(2,1)}, u32[]{:S(2)}) %copy-start) | copy-done | bytes 4194328
  39.8 5.9 %attend_near.1 = bf16[2240,128]{1,0:T(8,128)(2,1)} custom-call(s32[2]{0:T(128)S(1)} %pad_add_fusion.flags, bf16[2192,128]{1,0:T(8,128)(2,1)S(1)} %collective-permute-done.refs_0_, bf16[2,2,8,512,128]{4,3,2,1,0:T(8,128)(2,1)S(1)} %bitcast.16, bf16[2,2,8,512,128]{4,3,2,1,0:T(8,128)(2,1)S(1)} %bitcast.17, bf16[2,8,512,128]{3,2,1,0:T(8,128)(2,1)} %collective-permute-done.1.refs_3_), custom_call_target="tpu_custom_call" | custom-call | flops 1000 | bytes 1000 | tf_op jit(solution)/shard_map/attend_near/pallas_call | solution.py:215
  45.6 3.6 %collective-permute-start.2 = (bf16[2240,128]{1,0:T(8,128)(2,1)}, bf16[2240,128]{1,0:T(8,128)(2,1)S(1)}, u32[]{:S(2)}, u32[]{:S(2)}) collective-permute-start(bf16[2240,128]{1,0:T(8,128)(2,1)} %attend_near.1), channel_id=1, source_target_pairs={{0,2},{1,3},{2,4},{3,5},{4,6},{5,7},{6,8},{7,9},{8,10},{9,11},{10,... | collective-permute-start | bytes 1720328 | tf_op jit(solution)/shard_map/ppermute | solution.py:309
  49.3 0.0 collective-permute-done.3.refs_0_
  49.3 4.9 %attend_far.1.here_ref = bf16[2240,128]{1,0:T(8,128)(2,1)S(1)} custom-call(s32[2]{0:T(128)S(1)} %pad_add_fusion.flags, bf16[2192,128]{1,0:T(8,128)(2,1)} %collective-permute-done.3.refs_0_, bf16[2192,128]{1,0:T(8,128)(2,1)} %get-tuple-element.20.refs_0_.refs_1_, bf16[2,2,8,512,128]{4,3,2,1,0:T(8,128)(2,1)S(1)} %bitcast.18, ...), custom_call_target="tpu_custom_call" | custom-call | flops 1000 | bytes 1000 | tf_op jit(solution)/shard_map/attend_far/pallas_call | solution.py:215
  54.2 5.8 %collective-permute-start.4 = (bf16[2240,128]{1,0:T(8,128)(2,1)S(1)}, bf16[2240,128]{1,0:T(8,128)(2,1)}, u32[]{:S(2)}, u32[]{:S(2)}) collective-permute-start(bf16[2240,128]{1,0:T(8,128)(2,1)S(1)} %attend_far.1.here_ref), channel_id=1, source_target_pairs={{0,4},{2,6},{4,8},{6,10},{8,12},{10,14},{12,16},{14,18},{16,20},{1... | collective-permute-start | bytes 1720328 | tf_op jit(solution)/shard_map/ppermute | solution.py:309
  60.0 0.4 copy.18.slots_ref
  60.3 5.7 %collective-permute-done.2.back_ref.near_ref = bf16[2240,128]{1,0:T(8,128)(2,1)S(1)} collective-permute-done((bf16[2240,128]{1,0:T(8,128)(2,1)}, bf16[2240,128]{1,0:T(8,128)(2,1)S(1)}, u32[]{:S(2)}, u32[]{:S(2)}) %collective-permute-start.2) | collective-permute-done | bytes 573472 | tf_op jit(solution)/shard_map/ppermute | solution.py:309
  66.0 0.9 mix_early.1
  67.0 22.2 %collective-permute-done.4.far_ref = bf16[2240,128]{1,0:T(8,128)(2,1)} collective-permute-done((bf16[2240,128]{1,0:T(8,128)(2,1)S(1)}, bf16[2240,128]{1,0:T(8,128)(2,1)}, u32[]{:S(2)}, u32[]{:S(2)}) %collective-permute-start.4) | collective-permute-done | bytes 573472 | tf_op jit(solution)/shard_map/ppermute | solution.py:309
  89.2 4.8 %finish.1 = bf16[2048,128]{1,0:T(8,128)(2,1)} custom-call(s32[2]{0:T(128)S(1)} %pad_add_fusion.flags, bf16[2176,128]{1,0:T(8,128)(2,1)S(1)} %get-tuple-element.22.sum_ref, f32[24,128]{1,0:T(8,128)S(1)} %get-tuple-element.23.lines_ref, bf16[2240,128]{1,0:T(8,128)(2,1)S(1)} %collective-permute-done.2.back_ref.near_ref, ...), custom_call_target="tpu_custom_call" | custom-call | flops 1000 | bytes 1000 | tf_op jit(solution)/shard_map/finish/pallas_call | solution.py:295
Async XLA Ops:
  6.5 31.0 %all-gather.3.cloned.1.call-start = ((), (), s32[]{:S(2)}) async-start(), calls=%async_computation | async-start | bytes 6291456 | tf_op jit(solution)/shard_map/all_gather | solution.py:328
  8.5 5.1 %copy-start.3 = (bf16[256,8,128]{2,1,0:T(8,128)(2,1)S(1)}, bf16[256,8,128]{2,1,0:T(8,128)(2,1)}, u32[]{:S(2)}) copy-start(bf16[256,8,128]{2,1,0:T(8,128)(2,1)} %param.4) | copy-start | bytes 1572868
  10.0 1.6 %copy-start.1 = (bf16[2,8,512,128]{3,2,1,0:T(8,128)(2,1)S(1)}, bf16[2,8,512,128]{3,2,1,0:T(8,128)(2,1)}, u32[]{:S(2)}) copy-start(bf16[2,8,512,128]{3,2,1,0:T(8,128)(2,1)} %pad_maximum_fusion.refs_1_) | copy-start | bytes 6291460
  10.0 3.7 %copy-start.2 = (s32[256,8]{0,1:T(8,128)S(1)}, s32[256,8]{0,1:T(8,128)}, u32[]{:S(2)}) copy-start(s32[256,8]{0,1:T(8,128)} %param.7) | copy-start | bytes 24580
  11.6 25.9 %collective-permute-start.1 = (bf16[2,8,512,128]{3,2,1,0:T(8,128)(2,1)S(1)}, bf16[2,8,512,128]{3,2,1,0:T(8,128)(2,1)}, u32[]{:S(2)}, u32[]{:S(2)}) collective-permute-start(bf16[2,8,512,128]{3,2,1,0:T(8,128)(2,1)S(1)} %copy-done.1), channel_id=1, source_target_pairs={{1,3},{3,5},{5,7},{7,9},{9,11},{11,13},{13,15},{15,17},{17,19},{19... | collective-permute-start | bytes 6291464 | tf_op jit(solution)/shard_map/ppermute | solution.py:309
  17.6 20.0 %collective-permute-start = (bf16[2192,128]{1,0:T(8,128)(2,1)}, bf16[2192,128]{1,0:T(8,128)(2,1)S(1)}, u32[]{:S(2)}, u32[]{:S(2)}) collective-permute-start(bf16[2192,128]{1,0:T(8,128)(2,1)} %get-tuple-element.20.refs_0_.refs_1_), channel_id=1, source_target_pairs={{2,0},{3,1},{4,2},{5,3},{6,4},{7,5},{8,6},{9,7},{10,8},{11,9},{12,... | collective-permute-start | bytes 1683464 | tf_op jit(solution)/shard_map/ppermute | solution.py:309
  24.0 25.3 %collective-permute-start.3 = (bf16[2192,128]{1,0:T(8,128)(2,1)}, bf16[2192,128]{1,0:T(8,128)(2,1)}, u32[]{:S(2)}, u32[]{:S(2)}) collective-permute-start(bf16[2192,128]{1,0:T(8,128)(2,1)} %get-tuple-element.20.refs_0_.refs_1_), channel_id=1, source_target_pairs={{4,0},{6,2},{8,4},{10,6},{12,8},{14,10},{16,12},{18,14},{20,16},{2... | collective-permute-start | bytes 1683464 | tf_op jit(solution)/shard_map/ppermute | solution.py:309
  37.6 2.2 %copy-start = (bf16[4,8,512,128]{3,2,1,0:T(8,128)(2,1)S(1)}, bf16[4,8,512,128]{3,2,1,0:T(8,128)(2,1)}, u32[]{:S(2)}) copy-start(bf16[4,8,512,128]{3,2,1,0:T(8,128)(2,1)} %all-gather.3.cloned.1.call-done) | copy-start | bytes 12582916
  45.6 20.4 %collective-permute-start.2 = (bf16[2240,128]{1,0:T(8,128)(2,1)}, bf16[2240,128]{1,0:T(8,128)(2,1)S(1)}, u32[]{:S(2)}, u32[]{:S(2)}) collective-permute-start(bf16[2240,128]{1,0:T(8,128)(2,1)} %attend_near.1), channel_id=1, source_target_pairs={{0,2},{1,3},{2,4},{3,5},{4,6},{5,7},{6,8},{7,9},{8,10},{9,11},{10,... | collective-permute-start | bytes 1720328 | tf_op jit(solution)/shard_map/ppermute | solution.py:309
  54.2 35.0 %collective-permute-start.4 = (bf16[2240,128]{1,0:T(8,128)(2,1)S(1)}, bf16[2240,128]{1,0:T(8,128)(2,1)}, u32[]{:S(2)}, u32[]{:S(2)}) collective-permute-start(bf16[2240,128]{1,0:T(8,128)(2,1)S(1)} %attend_far.1.here_ref), channel_id=1, source_target_pairs={{0,4},{2,6},{4,8},{6,10},{8,12},{10,14},{12,16},{14,18},{16,20},{1... | collective-permute-start | bytes 1720328 | tf_op jit(solution)/shard_map/ppermute | solution.py:309
Sparse Core Ops, SparseCore 0:
  10.2 25.1 all-gather.2

commit v4 on v2

--- a/solution.py
+++ b/solution.py
@@ -88,9 +88,8 @@
     )(routes_t, queries_r)
 
 
-def attend_kernel(kind, flags, *refs):
-    q_count, kv_count = {"own": (1, 1), "near": (1, 3), "far": (2, 2)}[kind]
-    q_refs, refs = refs[:q_count], refs[q_count:]
+def attend_kernel(kind, flags, q_ref, *refs):
+    kv_count = {"own": 1, "near": 3, "far": 2}[kind]
     kv, refs = refs[:kv_count], refs[kv_count:]
     if kind == "own":
         pos_ref, out_ref, qs, os, ls, tail, starts, ps = refs
@@ -117,10 +116,7 @@
     def work(is_odd):
         @pl.when(step == 0)
         def _():
-            if kind == "far" and is_odd:
-                pltpu.sync_copy(q_refs[1], qs.at[pl.ds(0, ROWS + META)])
-            else:
-                qs[: ROWS + META] = q_refs[0][...]
+            qs[: ROWS + META] = q_ref[...]
             os[...] = jnp.zeros_like(os)
             ls[...] = jnp.zeros_like(ls)
             firsts = qs[ROWS : ROWS + META].astype(F32)
@@ -200,9 +196,8 @@
         return pl.BlockSpec((rows, 128), lambda g: (0, 0))
 
     in_specs = [pl.BlockSpec(memory_space=pltpu.SMEM)]
-    in_specs += [whole(ROWS + META)] + [pl.BlockSpec(memory_space=pltpu.HBM)] * (len(packed) - 1)
-    in_specs += [kv_spec] * len(kvs)
-    args = [flags, *packed, *kvs]
+    in_specs += [whole(ROWS + META)] + [kv_spec] * len(kvs)
+    args = [flags, packed, *kvs]
     scratch = [pltpu.VMEM((SPAN, 128), BF16), pltpu.VMEM((SPAN, 128), BF16), pltpu.VMEM((SPAN, 128), F32)]
     scratch += [pltpu.VMEM((TAIL, 128), F32), pltpu.SMEM((GROUPS,), I32)]
     if kind == "own":
@@ -302,7 +297,7 @@
 
 def moved(block, distance):
     devices = range(lax.axis_size("seq"))
-    pairs = [(i, i + distance(i)) for i in devices if distance(i) and i + distance(i) in devices]
+    pairs = [(i, i + distance(i)) for i in devices if distance(i) is not None and i + distance(i) in devices]
     return lax.ppermute(block, "seq", pairs)
 
 
@@ -316,19 +311,19 @@
         return lax.optimization_barrier((x, *others))[0]
 
     kv = jnp.stack([keys.transpose(1, 0, 2), values.transpose(1, 0, 2)])
-    kv_forward = moved(kv, lambda i: 2 if i % 2 else 0)
+    kv_forward = moved(kv, lambda i: 2 if i % 2 else None)
     packed, pos, slots = sort_queries(after(routes.T, kv), queries.transpose(1, 0, 2).reshape(-1, width))
     column = slots.T.reshape(-1, 1)
     near_q = moved(packed, lambda i: -2)
-    own = attend("own", flags, [packed], [kv], pos)
+    own = attend("own", flags, packed, [kv], pos)
     kv_sibling = moved(kv, lambda i: -1 if i % 2 else 1)
     far_q = moved(after(packed, own, column), lambda i: 0 if i % 2 else -4)
     near_q = after(near_q, own)
-    near_out = attend("near", flags, [near_q], [kv, kv_sibling, kv_forward])
+    near_out = attend("near", flags, near_q, [kv, kv_sibling, kv_forward])
     near_back = moved(near_out, lambda i: 2)
     far_q = after(far_q, near_out)
-    far_out = attend("far", flags, [far_q, packed], [kv, kv_sibling])
-    far_back = moved(far_out, lambda i: 0 if i % 2 else 4)
+    far_out = attend("far", flags, far_q, [kv, kv_sibling])
+    far_back = moved(far_out, lambda i: None if i % 2 else 4)
     early_sum, early_lines = mix_early(flags, own, near_back, far_out)
     out = finish(flags, early_sum, early_lines, near_back, after(far_back, early_sum), column)
     return out.reshape(tokens, routed, width)

time: 86.2 us -> 86.4 us (level)
  Pallas kernels: 24.2 us -> 25.4 us
  local copies, waits for them, and re-layouts: 3.66 us -> 2.61 us
  starting transfers between devices: 27.9 us -> 27 us
  waiting for transfers between devices: 29.6 us -> 30.5 us
    unnamed x8 -> x4, local copies, waits for them, and re-layouts: 1.07 us -> 0.01 us
    ppermute x6, starting transfers between devices: 27.9 us -> 27 us  [moved(): return lax.ppermute(block, 'seq', pairs)]
  transfers between devices with their start and end apart: 6 -> 6, of which waited for: 3 -> 3; matrix products, arithmetic and copies ran while one was open for 1% -> 1% of each run, Pallas kernels for 23% -> 24%
where the time goes in v4:
time: 86.4 us; the launch traced here: 85.9 us
  waiting for transfers between devices  30.5 us (35%)
  starting transfers between devices  27 us (31%)
  Pallas kernels  25.4 us (29%)
  local copies, waits for them, and re-layouts  2.61 us (3%)
    ppermute x6, waiting for transfers between devices, moved(): return lax.ppermute(block, 'seq', pairs)  30.5 us
    ppermute x6, starting transfers between devices, moved(): return lax.ppermute(block, 'seq', pairs)  27 us
    pallas_call x3, Pallas kernels, attend(): pl.pallas_call(functools.partial(attend_kernel, kind), grid=(GROUPS // ST...  15.3 us
    pallas_call x1, Pallas kernels, finish(): pl.pallas_call(finish_kernel, in_specs=[pl.BlockSpec(memory_space=pltpu.S...  4.81 us
    pallas_call x1, Pallas kernels, sort_queries(): pl.pallas_call(sort_kernel, out_shape=[jax.ShapeDtypeStruct((ROWS + META,...  3.85 us
    another operation x1, local copies, waits for them, and re-layouts, shards(): kv = jnp.stack([keys.transpose(1, 0, 2), values.transpose(1, 0, 2)])  1.92 us
  transfers between devices with their start and end apart: 6, of which 3 were waited for; matrix products, arithmetic and copies ran while one was open for 1% of the time, Pallas kernels for 24%

profile of v4, /device:TPU:120, one launch (start us, length us, event | category | flops | bytes accessed | tf_op | source)
XLA Modules:
  0.0 85.9 jit_solution(4674150634480068581)
XLA Ops:
  0.0 1.9 %copy_bitcast_fusion = (bf16[1,8,512,128]{3,2,1,0:T(8,128)(2,1)S(1)}, bf16[1,8,512,128]{3,2,1,0:T(8,128)(2,1)S(1)}) fusion(bf16[512,8,128]{2,1,0:T(8,128)(2,1)} %param.6, bf16[512,8,128]{2,1,0:T(8,128)(2,1)} %param.5), kind=kLoop, calls=%fused_computation.1 | loop fusion | bytes 4194304 | tf_op jit(solution)/shard_map/stack | solution.py:313
  1.9 0.0 copy-start.1
  1.9 0.0 copy-start
  2.0 0.2 pad_maximum_fusion.refs_0_
  2.2 1.9 %collective-permute-start.1 = (bf16[2,8,512,128]{3,2,1,0:T(8,128)(2,1)S(1)}, bf16[2,8,512,128]{3,2,1,0:T(8,128)(2,1)}, u32[]{:S(2)}, u32[]{:S(2)}) collective-permute-start(bf16[2,8,512,128]{3,2,1,0:T(8,128)(2,1)S(1)} %pad_maximum_fusion.refs_0_), channel_id=1, source_target_pairs={{0,1},{1,0},{2,3},{3,2},{4,5},{5,4},{6,7},{7,6},{8,9},{9,8},{10,11... | collective-permute-start | bytes 6291464 | tf_op jit(solution)/shard_map/ppermute | solution.py:301
  4.1 2.0 %collective-permute-start.2 = (bf16[2,8,512,128]{3,2,1,0:T(8,128)(2,1)S(1)}, bf16[2,8,512,128]{3,2,1,0:T(8,128)(2,1)}, u32[]{:S(2)}, u32[]{:S(2)}) collective-permute-start(bf16[2,8,512,128]{3,2,1,0:T(8,128)(2,1)S(1)} %pad_maximum_fusion.refs_0_), channel_id=1, source_target_pairs={{1,3},{3,5},{5,7},{7,9},{9,11},{11,13},{13,15},{15,17},{17,19},{19... | collective-permute-start | bytes 6291464 | tf_op jit(solution)/shard_map/ppermute | solution.py:301
  6.1 0.0 copy-done.1
  6.1 0.1 copy.11
  6.2 0.0 copy-done
  6.2 3.9 %sort_queries.1 = (bf16[2192,128]{1,0:T(8,128)(2,1)}, f32[24,128]{1,0:T(8,128)S(1)}, s32[8,256]{1,0:T(8,128)S(1)}) custom-call(s32[8,256]{1,0:T(8,128)S(1)} %bitcast.16, bf16[2048,128]{1,0:T(8,128)(2,1)S(1)} %bitcast.15), custom_call_target="tpu_custom_call" | custom-call | flops 1000 | bytes 1000 | tf_op jit(solution)/shard_map/sort_queries/pallas_call | solution.py:77
  10.0 1.9 %collective-permute-start = (bf16[2192,128]{1,0:T(8,128)(2,1)}, bf16[2192,128]{1,0:T(8,128)(2,1)S(1)}, u32[]{:S(2)}, u32[]{:S(2)}) collective-permute-start(bf16[2192,128]{1,0:T(8,128)(2,1)} %get-tuple-element.20.q_ref), channel_id=1, source_target_pairs={{2,0},{3,1},{4,2},{5,3},{6,4},{7,5},{8,6},{9,7},{10,8},{11,9},{12,... | collective-permute-start | bytes 1683464 | tf_op jit(solution)/shard_map/ppermute | solution.py:301
  11.9 0.1 pad_add_fusion.flags
  12.0 4.1 %attend_own.1.own_ref = bf16[2240,128]{1,0:T(8,128)(2,1)S(1)} custom-call(s32[2]{0:T(128)S(1)} %pad_add_fusion.flags, bf16[2192,128]{1,0:T(8,128)(2,1)} %get-tuple-element.20.q_ref, bf16[2,8,512,128]{3,2,1,0:T(8,128)(2,1)S(1)} %pad_maximum_fusion.refs_0_, f32[24,128]{1,0:T(8,128)S(1)} %get-tuple-element.17.refs_1_), custom_call_target="tpu_custom_call" | custom-call | flops 1000 | bytes 1000 | tf_op jit(solution)/shard_map/attend_own/pallas_call | solution.py:207
  16.2 0.1 copy.12
  16.3 0.1 reshape.10
  16.4 13.6 %collective-permute-start.4 = (bf16[2192,128]{1,0:T(8,128)(2,1)}, bf16[2192,128]{1,0:T(8,128)(2,1)S(1)}, u32[]{:S(2)}, u32[]{:S(2)}) collective-permute-start(bf16[2192,128]{1,0:T(8,128)(2,1)} %get-tuple-element.20.q_ref), channel_id=1, source_target_pairs={{1,1},{3,3},{4,0},{5,5},{6,2},{7,7},{8,4},{9,9},{10,6},{11,11},{12... | collective-permute-start | bytes 1683464 | tf_op jit(solution)/shard_map/ppermute | solution.py:301
  30.0 0.0 collective-permute-done.q_ref
  30.0 0.0 collective-permute-done.1.refs_1_
  30.0 0.0 collective-permute-done.2.refs_2_
  30.0 6.1 %attend_near.1 = bf16[2240,128]{1,0:T(8,128)(2,1)} custom-call(s32[2]{0:T(128)S(1)} %pad_add_fusion.flags, bf16[2192,128]{1,0:T(8,128)(2,1)S(1)} %collective-permute-done.q_ref, bf16[2,8,512,128]{3,2,1,0:T(8,128)(2,1)S(1)} %pad_maximum_fusion.refs_0_, bf16[2,8,512,128]{3,2,1,0:T(8,128)(2,1)} %collective-permute-done.1.refs_1_, ...), custom_call_target="tpu_custom_call" | custom-call | flops 1000 | bytes 1000 | tf_op jit(solution)/shard_map/attend_near/pallas_call | solution.py:207
  36.2 3.5 %collective-permute-start.3 = (bf16[2240,128]{1,0:T(8,128)(2,1)}, bf16[2240,128]{1,0:T(8,128)(2,1)}, u32[]{:S(2)}, u32[]{:S(2)}) collective-permute-start(bf16[2240,128]{1,0:T(8,128)(2,1)} %attend_near.1), channel_id=1, source_target_pairs={{0,2},{1,3},{2,4},{3,5},{4,6},{5,7},{6,8},{7,9},{8,10},{9,11},{10,... | collective-permute-start | bytes 1720328 | tf_op jit(solution)/shard_map/ppermute | solution.py:301
  39.7 1.3 %collective-permute-done.4.q_ref = bf16[2192,128]{1,0:T(8,128)(2,1)S(1)} collective-permute-done((bf16[2192,128]{1,0:T(8,128)(2,1)}, bf16[2192,128]{1,0:T(8,128)(2,1)S(1)}, u32[]{:S(2)}, u32[]{:S(2)}) %collective-permute-start.4) | collective-permute-done | bytes 561184 | tf_op jit(solution)/shard_map/ppermute | solution.py:301
  41.0 5.0 %attend_far.1.here_ref = bf16[2240,128]{1,0:T(8,128)(2,1)S(1)} custom-call(s32[2]{0:T(128)S(1)} %pad_add_fusion.flags, bf16[2192,128]{1,0:T(8,128)(2,1)S(1)} %collective-permute-done.4.q_ref, bf16[2,8,512,128]{3,2,1,0:T(8,128)(2,1)S(1)} %pad_maximum_fusion.refs_0_, bf16[2,8,512,128]{3,2,1,0:T(8,128)(2,1)} %collective-permute-done.1.refs_1_), custom_call_target="tpu_custom_call" | custom-call | flops 1000 | bytes 1000 | tf_op jit(solution)/shard_map/attend_far/pallas_call | solution.py:207
  46.0 4.0 %collective-permute-start.5 = (bf16[2240,128]{1,0:T(8,128)(2,1)S(1)}, bf16[2240,128]{1,0:T(8,128)(2,1)S(1)}, u32[]{:S(2)}, u32[]{:S(2)}) collective-permute-start(bf16[2240,128]{1,0:T(8,128)(2,1)S(1)} %attend_far.1.here_ref), channel_id=1, source_target_pairs={{0,4},{2,6},{4,8},{6,10},{8,12},{10,14},{12,16},{14,18},{16,20},{1... | collective-permute-start | bytes 1720328 | tf_op jit(solution)/shard_map/ppermute | solution.py:301
  50.0 0.4 copy.13.slots_ref
  50.4 8.6 %collective-permute-done.3.back_ref.near_ref = bf16[2240,128]{1,0:T(8,128)(2,1)} collective-permute-done((bf16[2240,128]{1,0:T(8,128)(2,1)}, bf16[2240,128]{1,0:T(8,128)(2,1)}, u32[]{:S(2)}, u32[]{:S(2)}) %collective-permute-start.3) | collective-permute-done | bytes 573472 | tf_op jit(solution)/shard_map/ppermute | solution.py:301
  59.0 1.5 %mix_early.1 = (bf16[2176,128]{1,0:T(8,128)(2,1)S(1)}, f32[24,128]{1,0:T(8,128)S(1)}) custom-call(s32[2]{0:T(128)S(1)} %pad_add_fusion.flags, bf16[2240,128]{1,0:T(8,128)(2,1)S(1)} %attend_own.1.own_ref, bf16[2240,128]{1,0:T(8,128)(2,1)} %collective-permute-done.3.back_ref.near_ref, bf16[2240,128]{1,0:T(8,128)(2,1)S(1)} %attend_far.1.here_ref), custom_call_target="tpu_custom_call" | custom-call | flops 1000 | bytes 1000 | tf_op jit(solution)/shard_map/mix_early/pallas_call | solution.py:255
  60.4 20.6 %collective-permute-done.5.far_ref = bf16[2240,128]{1,0:T(8,128)(2,1)S(1)} collective-permute-done((bf16[2240,128]{1,0:T(8,128)(2,1)S(1)}, bf16[2240,128]{1,0:T(8,128)(2,1)S(1)}, u32[]{:S(2)}, u32[]{:S(2)}) %collective-permute-start.5) | collective-permute-done | bytes 573472 | tf_op jit(solution)/shard_map/ppermute | solution.py:301
  81.1 4.8 %finish.1 = bf16[2048,128]{1,0:T(8,128)(2,1)} custom-call(s32[2]{0:T(128)S(1)} %pad_add_fusion.flags, bf16[2176,128]{1,0:T(8,128)(2,1)S(1)} %get-tuple-element.22.sum_ref, f32[24,128]{1,0:T(8,128)S(1)} %get-tuple-element.23.lines_ref, bf16[2240,128]{1,0:T(8,128)(2,1)} %collective-permute-done.3.back_ref.near_ref, ...), custom_call_target="tpu_custom_call" | custom-call | flops 1000 | bytes 1000 | tf_op jit(solution)/shard_map/finish/pallas_call | solution.py:287
Async XLA Ops:
  1.9 4.2 %copy-start.1 = (bf16[256,8,128]{2,1,0:T(8,128)(2,1)S(1)}, bf16[256,8,128]{2,1,0:T(8,128)(2,1)}, u32[]{:S(2)}) copy-start(bf16[256,8,128]{2,1,0:T(8,128)(2,1)} %param.4) | copy-start | bytes 1572868
  1.9 4.2 %copy-start = (s32[256,8]{0,1:T(8,128)S(1)}, s32[256,8]{0,1:T(8,128)}, u32[]{:S(2)}) copy-start(s32[256,8]{0,1:T(8,128)} %param.7) | copy-start | bytes 24580
  2.2 27.9 %collective-permute-start.1 = (bf16[2,8,512,128]{3,2,1,0:T(8,128)(2,1)S(1)}, bf16[2,8,512,128]{3,2,1,0:T(8,128)(2,1)}, u32[]{:S(2)}, u32[]{:S(2)}) collective-permute-start(bf16[2,8,512,128]{3,2,1,0:T(8,128)(2,1)S(1)} %pad_maximum_fusion.refs_0_), channel_id=1, source_target_pairs={{0,1},{1,0},{2,3},{3,2},{4,5},{5,4},{6,7},{7,6},{8,9},{9,8},{10,11... | collective-permute-start | bytes 6291464 | tf_op jit(solution)/shard_map/ppermute | solution.py:301
  4.1 25.9 %collective-permute-start.2 = (bf16[2,8,512,128]{3,2,1,0:T(8,128)(2,1)S(1)}, bf16[2,8,512,128]{3,2,1,0:T(8,128)(2,1)}, u32[]{:S(2)}, u32[]{:S(2)}) collective-permute-start(bf16[2,8,512,128]{3,2,1,0:T(8,128)(2,1)S(1)} %pad_maximum_fusion.refs_0_), channel_id=1, source_target_pairs={{1,3},{3,5},{5,7},{7,9},{9,11},{11,13},{13,15},{15,17},{17,19},{19... | collective-permute-start | bytes 6291464 | tf_op jit(solution)/shard_map/ppermute | solution.py:301
  10.0 20.0 %collective-permute-start = (bf16[2192,128]{1,0:T(8,128)(2,1)}, bf16[2192,128]{1,0:T(8,128)(2,1)S(1)}, u32[]{:S(2)}, u32[]{:S(2)}) collective-permute-start(bf16[2192,128]{1,0:T(8,128)(2,1)} %get-tuple-element.20.q_ref), channel_id=1, source_target_pairs={{2,0},{3,1},{4,2},{5,3},{6,4},{7,5},{8,6},{9,7},{10,8},{11,9},{12,... | collective-permute-start | bytes 1683464 | tf_op jit(solution)/shard_map/ppermute | solution.py:301
  16.4 24.5 %collective-permute-start.4 = (bf16[2192,128]{1,0:T(8,128)(2,1)}, bf16[2192,128]{1,0:T(8,128)(2,1)S(1)}, u32[]{:S(2)}, u32[]{:S(2)}) collective-permute-start(bf16[2192,128]{1,0:T(8,128)(2,1)} %get-tuple-element.20.q_ref), channel_id=1, source_target_pairs={{1,1},{3,3},{4,0},{5,5},{6,2},{7,7},{8,4},{9,9},{10,6},{11,11},{12... | collective-permute-start | bytes 1683464 | tf_op jit(solution)/shard_map/ppermute | solution.py:301
  36.2 22.8 %collective-permute-start.3 = (bf16[2240,128]{1,0:T(8,128)(2,1)}, bf16[2240,128]{1,0:T(8,128)(2,1)}, u32[]{:S(2)}, u32[]{:S(2)}) collective-permute-start(bf16[2240,128]{1,0:T(8,128)(2,1)} %attend_near.1), channel_id=1, source_target_pairs={{0,2},{1,3},{2,4},{3,5},{4,6},{5,7},{6,8},{7,9},{8,10},{9,11},{10,... | collective-permute-start | bytes 1720328 | tf_op jit(solution)/shard_map/ppermute | solution.py:301
  46.0 35.1 %collective-permute-start.5 = (bf16[2240,128]{1,0:T(8,128)(2,1)S(1)}, bf16[2240,128]{1,0:T(8,128)(2,1)S(1)}, u32[]{:S(2)}, u32[]{:S(2)}) collective-permute-start(bf16[2240,128]{1,0:T(8,128)(2,1)S(1)} %attend_far.1.here_ref), channel_id=1, source_target_pairs={{0,4},{2,6},{4,8},{6,10},{8,12},{10,14},{12,16},{14,18},{16,20},{1... | collective-permute-start | bytes 1720328 | tf_op jit(solution)/shard_map/ppermute | solution.py:301

commit v5 on v4

--- a/solution.py
+++ b/solution.py
@@ -276,9 +276,9 @@
     pl.when(odd == 1)(lambda: merge(near_ref, chip >= 1))
     pl.when(odd == 0)(lambda: merge(far_ref, chip >= 2))
     entries = out_ref.shape[0]
-    for e in range(entries // 256):
-        rows = slice(e * 256, (e + 1) * 256)
-        place = one_hot(iota((256, ROWS), 1) == slots_ref[rows])
+    for e in range(entries // 512):
+        rows = slice(e * 512, (e + 1) * 512)
+        place = one_hot(iota((512, ROWS), 1) == slots_ref[rows])
         out_ref[rows] = dot(place, merged[...]).astype(BF16)
 
 

time: 86.4 us -> 86.3 us (level)
  the two profiles are of different devices: /device:TPU:120 before, /device:TPU:112 now
where the time goes in v5:
time: 86.3 us; the launch traced here: 85.9 us
  waiting for transfers between devices  30.5 us (35%)
  starting transfers between devices  27 us (31%)
  Pallas kernels  25.4 us (29%)
  local copies, waits for them, and re-layouts  2.61 us (3%)
    ppermute x6, waiting for transfers between devices, moved(): return lax.ppermute(block, 'seq', pairs)  30.5 us
    ppermute x6, starting transfers between devices, moved(): return lax.ppermute(block, 'seq', pairs)  27 us
    pallas_call x3, Pallas kernels, attend(): pl.pallas_call(functools.partial(attend_kernel, kind), grid=(GROUPS // ST...  15.3 us
    pallas_call x1, Pallas kernels, finish(): pl.pallas_call(finish_kernel, in_specs=[pl.BlockSpec(memory_space=pltpu.S...  4.78 us
    pallas_call x1, Pallas kernels, sort_queries(): pl.pallas_call(sort_kernel, out_shape=[jax.ShapeDtypeStruct((ROWS + META,...  3.85 us
    another operation x1, local copies, waits for them, and re-layouts, shards(): kv = jnp.stack([keys.transpose(1, 0, 2), values.transpose(1, 0, 2)])  1.92 us
  transfers between devices with their start and end apart: 6, of which 3 were waited for; matrix products, arithmetic and copies ran while one was open for 1% of the time, Pallas kernels for 24%

profile of v5, /device:TPU:112, one launch (start us, length us, event | category | flops | bytes accessed | tf_op | source)
XLA Modules:
  0.0 85.9 jit_solution(7796111988570081684)
XLA Ops:
  0.0 1.9 %copy_bitcast_fusion = (bf16[1,8,512,128]{3,2,1,0:T(8,128)(2,1)S(1)}, bf16[1,8,512,128]{3,2,1,0:T(8,128)(2,1)S(1)}) fusion(bf16[512,8,128]{2,1,0:T(8,128)(2,1)} %param.6, bf16[512,8,128]{2,1,0:T(8,128)(2,1)} %param.5), kind=kLoop, calls=%fused_computation.1 | loop fusion | bytes 4194304 | tf_op jit(solution)/shard_map/stack | solution.py:313
  1.9 0.0 copy-start.1
  1.9 0.0 copy-start
  2.0 0.2 pad_maximum_fusion.refs_0_
  2.2 1.9 %collective-permute-start.1 = (bf16[2,8,512,128]{3,2,1,0:T(8,128)(2,1)S(1)}, bf16[2,8,512,128]{3,2,1,0:T(8,128)(2,1)}, u32[]{:S(2)}, u32[]{:S(2)}) collective-permute-start(bf16[2,8,512,128]{3,2,1,0:T(8,128)(2,1)S(1)} %pad_maximum_fusion.refs_0_), channel_id=1, source_target_pairs={{0,1},{1,0},{2,3},{3,2},{4,5},{5,4},{6,7},{7,6},{8,9},{9,8},{10,11... | collective-permute-start | bytes 6291464 | tf_op jit(solution)/shard_map/ppermute | solution.py:301
  4.1 2.0 %collective-permute-start.2 = (bf16[2,8,512,128]{3,2,1,0:T(8,128)(2,1)S(1)}, bf16[2,8,512,128]{3,2,1,0:T(8,128)(2,1)}, u32[]{:S(2)}, u32[]{:S(2)}) collective-permute-start(bf16[2,8,512,128]{3,2,1,0:T(8,128)(2,1)S(1)} %pad_maximum_fusion.refs_0_), channel_id=1, source_target_pairs={{1,3},{3,5},{5,7},{7,9},{9,11},{11,13},{13,15},{15,17},{17,19},{19... | collective-permute-start | bytes 6291464 | tf_op jit(solution)/shard_map/ppermute | solution.py:301
  6.1 0.0 copy-done.1
  6.1 0.1 copy.11
  6.2 0.0 copy-done
  6.2 3.9 %sort_queries.1 = (bf16[2192,128]{1,0:T(8,128)(2,1)}, f32[24,128]{1,0:T(8,128)S(1)}, s32[8,256]{1,0:T(8,128)S(1)}) custom-call(s32[8,256]{1,0:T(8,128)S(1)} %bitcast.16, bf16[2048,128]{1,0:T(8,128)(2,1)S(1)} %bitcast.15), custom_call_target="tpu_custom_call" | custom-call | flops 1000 | bytes 1000 | tf_op jit(solution)/shard_map/sort_queries/pallas_call | solution.py:77
  10.0 1.9 %collective-permute-start = (bf16[2192,128]{1,0:T(8,128)(2,1)}, bf16[2192,128]{1,0:T(8,128)(2,1)S(1)}, u32[]{:S(2)}, u32[]{:S(2)}) collective-permute-start(bf16[2192,128]{1,0:T(8,128)(2,1)} %get-tuple-element.20.q_ref), channel_id=1, source_target_pairs={{2,0},{3,1},{4,2},{5,3},{6,4},{7,5},{8,6},{9,7},{10,8},{11,9},{12,... | collective-permute-start | bytes 1683464 | tf_op jit(solution)/shard_map/ppermute | solution.py:301
  11.9 0.1 pad_add_fusion.flags
  12.0 4.1 %attend_own.1.own_ref = bf16[2240,128]{1,0:T(8,128)(2,1)S(1)} custom-call(s32[2]{0:T(128)S(1)} %pad_add_fusion.flags, bf16[2192,128]{1,0:T(8,128)(2,1)} %get-tuple-element.20.q_ref, bf16[2,8,512,128]{3,2,1,0:T(8,128)(2,1)S(1)} %pad_maximum_fusion.refs_0_, f32[24,128]{1,0:T(8,128)S(1)} %get-tuple-element.17.refs_1_), custom_call_target="tpu_custom_call" | custom-call | flops 1000 | bytes 1000 | tf_op jit(solution)/shard_map/attend_own/pallas_call | solution.py:207
  16.2 0.1 copy.12
  16.3 0.1 reshape.10
  16.4 13.6 %collective-permute-start.4 = (bf16[2192,128]{1,0:T(8,128)(2,1)}, bf16[2192,128]{1,0:T(8,128)(2,1)S(1)}, u32[]{:S(2)}, u32[]{:S(2)}) collective-permute-start(bf16[2192,128]{1,0:T(8,128)(2,1)} %get-tuple-element.20.q_ref), channel_id=1, source_target_pairs={{1,1},{3,3},{4,0},{5,5},{6,2},{7,7},{8,4},{9,9},{10,6},{11,11},{12... | collective-permute-start | bytes 1683464 | tf_op jit(solution)/shard_map/ppermute | solution.py:301
  30.0 0.0 collective-permute-done.q_ref
  30.0 0.0 collective-permute-done.1.refs_1_
  30.0 0.0 collective-permute-done.2.refs_2_
  30.0 6.1 %attend_near.1 = bf16[2240,128]{1,0:T(8,128)(2,1)} custom-call(s32[2]{0:T(128)S(1)} %pad_add_fusion.flags, bf16[2192,128]{1,0:T(8,128)(2,1)S(1)} %collective-permute-done.q_ref, bf16[2,8,512,128]{3,2,1,0:T(8,128)(2,1)S(1)} %pad_maximum_fusion.refs_0_, bf16[2,8,512,128]{3,2,1,0:T(8,128)(2,1)} %collective-permute-done.1.refs_1_, ...), custom_call_target="tpu_custom_call" | custom-call | flops 1000 | bytes 1000 | tf_op jit(solution)/shard_map/attend_near/pallas_call | solution.py:207
  36.1 3.6 %collective-permute-start.3 = (bf16[2240,128]{1,0:T(8,128)(2,1)}, bf16[2240,128]{1,0:T(8,128)(2,1)}, u32[]{:S(2)}, u32[]{:S(2)}) collective-permute-start(bf16[2240,128]{1,0:T(8,128)(2,1)} %attend_near.1), channel_id=1, source_target_pairs={{0,2},{1,3},{2,4},{3,5},{4,6},{5,7},{6,8},{7,9},{8,10},{9,11},{10,... | collective-permute-start | bytes 1720328 | tf_op jit(solution)/shard_map/ppermute | solution.py:301
  39.7 1.2 %collective-permute-done.4.q_ref = bf16[2192,128]{1,0:T(8,128)(2,1)S(1)} collective-permute-done((bf16[2192,128]{1,0:T(8,128)(2,1)}, bf16[2192,128]{1,0:T(8,128)(2,1)S(1)}, u32[]{:S(2)}, u32[]{:S(2)}) %collective-permute-start.4) | collective-permute-done | bytes 561184 | tf_op jit(solution)/shard_map/ppermute | solution.py:301
  41.0 5.0 %attend_far.1.here_ref = bf16[2240,128]{1,0:T(8,128)(2,1)S(1)} custom-call(s32[2]{0:T(128)S(1)} %pad_add_fusion.flags, bf16[2192,128]{1,0:T(8,128)(2,1)S(1)} %collective-permute-done.4.q_ref, bf16[2,8,512,128]{3,2,1,0:T(8,128)(2,1)S(1)} %pad_maximum_fusion.refs_0_, bf16[2,8,512,128]{3,2,1,0:T(8,128)(2,1)} %collective-permute-done.1.refs_1_), custom_call_target="tpu_custom_call" | custom-call | flops 1000 | bytes 1000 | tf_op jit(solution)/shard_map/attend_far/pallas_call | solution.py:207
  46.0 4.0 %collective-permute-start.5 = (bf16[2240,128]{1,0:T(8,128)(2,1)S(1)}, bf16[2240,128]{1,0:T(8,128)(2,1)S(1)}, u32[]{:S(2)}, u32[]{:S(2)}) collective-permute-start(bf16[2240,128]{1,0:T(8,128)(2,1)S(1)} %attend_far.1.here_ref), channel_id=1, source_target_pairs={{0,4},{2,6},{4,8},{6,10},{8,12},{10,14},{12,16},{14,18},{16,20},{1... | collective-permute-start | bytes 1720328 | tf_op jit(solution)/shard_map/ppermute | solution.py:301
  50.0 0.4 copy.13.slots_ref
  50.4 8.6 %collective-permute-done.3.back_ref.near_ref = bf16[2240,128]{1,0:T(8,128)(2,1)} collective-permute-done((bf16[2240,128]{1,0:T(8,128)(2,1)}, bf16[2240,128]{1,0:T(8,128)(2,1)}, u32[]{:S(2)}, u32[]{:S(2)}) %collective-permute-start.3) | collective-permute-done | bytes 573472 | tf_op jit(solution)/shard_map/ppermute | solution.py:301
  59.0 1.5 %mix_early.1 = (bf16[2176,128]{1,0:T(8,128)(2,1)S(1)}, f32[24,128]{1,0:T(8,128)S(1)}) custom-call(s32[2]{0:T(128)S(1)} %pad_add_fusion.flags, bf16[2240,128]{1,0:T(8,128)(2,1)S(1)} %attend_own.1.own_ref, bf16[2240,128]{1,0:T(8,128)(2,1)} %collective-permute-done.3.back_ref.near_ref, bf16[2240,128]{1,0:T(8,128)(2,1)S(1)} %attend_far.1.here_ref), custom_call_target="tpu_custom_call" | custom-call | flops 1000 | bytes 1000 | tf_op jit(solution)/shard_map/mix_early/pallas_call | solution.py:255
  60.4 20.7 %collective-permute-done.5.far_ref = bf16[2240,128]{1,0:T(8,128)(2,1)S(1)} collective-permute-done((bf16[2240,128]{1,0:T(8,128)(2,1)S(1)}, bf16[2240,128]{1,0:T(8,128)(2,1)S(1)}, u32[]{:S(2)}, u32[]{:S(2)}) %collective-permute-start.5) | collective-permute-done | bytes 573472 | tf_op jit(solution)/shard_map/ppermute | solution.py:301
  81.1 4.8 %finish.1 = bf16[2048,128]{1,0:T(8,128)(2,1)} custom-call(s32[2]{0:T(128)S(1)} %pad_add_fusion.flags, bf16[2176,128]{1,0:T(8,128)(2,1)S(1)} %get-tuple-element.22.sum_ref, f32[24,128]{1,0:T(8,128)S(1)} %get-tuple-element.23.lines_ref, bf16[2240,128]{1,0:T(8,128)(2,1)} %collective-permute-done.3.back_ref.near_ref, ...), custom_call_target="tpu_custom_call" | custom-call | flops 1000 | bytes 1000 | tf_op jit(solution)/shard_map/finish/pallas_call | solution.py:287
Async XLA Ops:
  1.9 4.2 %copy-start.1 = (bf16[256,8,128]{2,1,0:T(8,128)(2,1)S(1)}, bf16[256,8,128]{2,1,0:T(8,128)(2,1)}, u32[]{:S(2)}) copy-start(bf16[256,8,128]{2,1,0:T(8,128)(2,1)} %param.4) | copy-start | bytes 1572868
  1.9 4.2 %copy-start = (s32[256,8]{0,1:T(8,128)S(1)}, s32[256,8]{0,1:T(8,128)}, u32[]{:S(2)}) copy-start(s32[256,8]{0,1:T(8,128)} %param.7) | copy-start | bytes 24580
  2.2 27.9 %collective-permute-start.1 = (bf16[2,8,512,128]{3,2,1,0:T(8,128)(2,1)S(1)}, bf16[2,8,512,128]{3,2,1,0:T(8,128)(2,1)}, u32[]{:S(2)}, u32[]{:S(2)}) collective-permute-start(bf16[2,8,512,128]{3,2,1,0:T(8,128)(2,1)S(1)} %pad_maximum_fusion.refs_0_), channel_id=1, source_target_pairs={{0,1},{1,0},{2,3},{3,2},{4,5},{5,4},{6,7},{7,6},{8,9},{9,8},{10,11... | collective-permute-start | bytes 6291464 | tf_op jit(solution)/shard_map/ppermute | solution.py:301
  4.1 25.9 %collective-permute-start.2 = (bf16[2,8,512,128]{3,2,1,0:T(8,128)(2,1)S(1)}, bf16[2,8,512,128]{3,2,1,0:T(8,128)(2,1)}, u32[]{:S(2)}, u32[]{:S(2)}) collective-permute-start(bf16[2,8,512,128]{3,2,1,0:T(8,128)(2,1)S(1)} %pad_maximum_fusion.refs_0_), channel_id=1, source_target_pairs={{1,3},{3,5},{5,7},{7,9},{9,11},{11,13},{13,15},{15,17},{17,19},{19... | collective-permute-start | bytes 6291464 | tf_op jit(solution)/shard_map/ppermute | solution.py:301
  10.0 20.0 %collective-permute-start = (bf16[2192,128]{1,0:T(8,128)(2,1)}, bf16[2192,128]{1,0:T(8,128)(2,1)S(1)}, u32[]{:S(2)}, u32[]{:S(2)}) collective-permute-start(bf16[2192,128]{1,0:T(8,128)(2,1)} %get-tuple-element.20.q_ref), channel_id=1, source_target_pairs={{2,0},{3,1},{4,2},{5,3},{6,4},{7,5},{8,6},{9,7},{10,8},{11,9},{12,... | collective-permute-start | bytes 1683464 | tf_op jit(solution)/shard_map/ppermute | solution.py:301
  16.4 24.5 %collective-permute-start.4 = (bf16[2192,128]{1,0:T(8,128)(2,1)}, bf16[2192,128]{1,0:T(8,128)(2,1)S(1)}, u32[]{:S(2)}, u32[]{:S(2)}) collective-permute-start(bf16[2192,128]{1,0:T(8,128)(2,1)} %get-tuple-element.20.q_ref), channel_id=1, source_target_pairs={{1,1},{3,3},{4,0},{5,5},{6,2},{7,7},{8,4},{9,9},{10,6},{11,11},{12... | collective-permute-start | bytes 1683464 | tf_op jit(solution)/shard_map/ppermute | solution.py:301
  36.1 22.8 %collective-permute-start.3 = (bf16[2240,128]{1,0:T(8,128)(2,1)}, bf16[2240,128]{1,0:T(8,128)(2,1)}, u32[]{:S(2)}, u32[]{:S(2)}) collective-permute-start(bf16[2240,128]{1,0:T(8,128)(2,1)} %attend_near.1), channel_id=1, source_target_pairs={{0,2},{1,3},{2,4},{3,5},{4,6},{5,7},{6,8},{7,9},{8,10},{9,11},{10,... | collective-permute-start | bytes 1720328 | tf_op jit(solution)/shard_map/ppermute | solution.py:301
  46.0 35.1 %collective-permute-start.5 = (bf16[2240,128]{1,0:T(8,128)(2,1)S(1)}, bf16[2240,128]{1,0:T(8,128)(2,1)S(1)}, u32[]{:S(2)}, u32[]{:S(2)}) collective-permute-start(bf16[2240,128]{1,0:T(8,128)(2,1)S(1)} %attend_far.1.here_ref), channel_id=1, source_target_pairs={{0,4},{2,6},{4,8},{6,10},{8,12},{10,14},{12,16},{14,18},{16,20},{1... | collective-permute-start | bytes 1720328 | tf_op jit(solution)/shard_map/ppermute | solution.py:301

commit v6 on v4

--- a/solution.py
+++ b/solution.py
@@ -317,7 +317,7 @@
     near_q = moved(packed, lambda i: -2)
     own = attend("own", flags, packed, [kv], pos)
     kv_sibling = moved(kv, lambda i: -1 if i % 2 else 1)
-    far_q = moved(after(packed, own, column), lambda i: 0 if i % 2 else -4)
+    far_q = moved(packed, lambda i: 0 if i % 2 else -4)
     near_q = after(near_q, own)
     near_out = attend("near", flags, near_q, [kv, kv_sibling, kv_forward])
     near_back = moved(near_out, lambda i: 2)

time: 86.4 us -> 88.7 us (1.027)
  the two profiles are of different devices: /device:TPU:120 before, /device:TPU:96 now
where the time goes in v6:
time: 88.7 us; the launch traced here: 88 us
  waiting for transfers between devices  31.1 us (35%)
  starting transfers between devices  28.4 us (32%)
  Pallas kernels  25.6 us (29%)
  local copies, waits for them, and re-layouts  2.44 us (3%)
    ppermute x6, waiting for transfers between devices, moved(): return lax.ppermute(block, 'seq', pairs)  31.1 us
    ppermute x6, starting transfers between devices, moved(): return lax.ppermute(block, 'seq', pairs)  28.4 us
    pallas_call x3, Pallas kernels, attend(): pl.pallas_call(functools.partial(attend_kernel, kind), grid=(GROUPS // ST...  15.4 us
    pallas_call x1, Pallas kernels, finish(): pl.pallas_call(finish_kernel, in_specs=[pl.BlockSpec(memory_space=pltpu.S...  4.81 us
    pallas_call x1, Pallas kernels, sort_queries(): pl.pallas_call(sort_kernel, out_shape=[jax.ShapeDtypeStruct((ROWS + META,...  3.87 us
    another operation x1, local copies, waits for them, and re-layouts, shards(): kv = jnp.stack([keys.transpose(1, 0, 2), values.transpose(1, 0, 2)])  1.92 us
  transfers between devices with their start and end apart: 6, of which 2 were waited for; matrix products, arithmetic and copies ran while one was open for 1% of the time, Pallas kernels for 24%

profile of v6, /device:TPU:96, one launch (start us, length us, event | category | flops | bytes accessed | tf_op | source)
XLA Modules:
  0.0 88.0 jit_solution(6166879427859801021)
XLA Ops:
  0.0 1.9 %copy_bitcast_fusion = (bf16[1,8,512,128]{3,2,1,0:T(8,128)(2,1)S(1)}, bf16[1,8,512,128]{3,2,1,0:T(8,128)(2,1)S(1)}) fusion(bf16[512,8,128]{2,1,0:T(8,128)(2,1)} %param.6, bf16[512,8,128]{2,1,0:T(8,128)(2,1)} %param.5), kind=kLoop, calls=%fused_computation.1 | loop fusion | bytes 4194304 | tf_op jit(solution)/shard_map/stack | solution.py:313
  1.9 0.0 copy-start.1
  1.9 0.0 copy-start
  2.0 0.2 pad_maximum_fusion.refs_0_
  2.2 1.9 %collective-permute-start.1 = (bf16[2,8,512,128]{3,2,1,0:T(8,128)(2,1)S(1)}, bf16[2,8,512,128]{3,2,1,0:T(8,128)(2,1)}, u32[]{:S(2)}, u32[]{:S(2)}) collective-permute-start(bf16[2,8,512,128]{3,2,1,0:T(8,128)(2,1)S(1)} %pad_maximum_fusion.refs_0_), channel_id=1, source_target_pairs={{0,1},{1,0},{2,3},{3,2},{4,5},{5,4},{6,7},{7,6},{8,9},{9,8},{10,11... | collective-permute-start | bytes 6291464 | tf_op jit(solution)/shard_map/ppermute | solution.py:301
  4.1 2.0 %collective-permute-start.2 = (bf16[2,8,512,128]{3,2,1,0:T(8,128)(2,1)S(1)}, bf16[2,8,512,128]{3,2,1,0:T(8,128)(2,1)}, u32[]{:S(2)}, u32[]{:S(2)}) collective-permute-start(bf16[2,8,512,128]{3,2,1,0:T(8,128)(2,1)S(1)} %pad_maximum_fusion.refs_0_), channel_id=1, source_target_pairs={{1,3},{3,5},{5,7},{7,9},{9,11},{11,13},{13,15},{15,17},{17,19},{19... | collective-permute-start | bytes 6291464 | tf_op jit(solution)/shard_map/ppermute | solution.py:301
  6.1 0.0 copy-done.1
  6.1 0.1 copy.11
  6.2 0.0 copy-done
  6.2 3.9 %sort_queries.1 = (bf16[2192,128]{1,0:T(8,128)(2,1)}, f32[24,128]{1,0:T(8,128)S(1)}, s32[8,256]{1,0:T(8,128)S(1)}) custom-call(s32[8,256]{1,0:T(8,128)S(1)} %bitcast.16, bf16[2048,128]{1,0:T(8,128)(2,1)S(1)} %bitcast.15), custom_call_target="tpu_custom_call" | custom-call | flops 1000 | bytes 1000 | tf_op jit(solution)/shard_map/sort_queries/pallas_call | solution.py:77
  10.0 1.9 %collective-permute-start = (bf16[2192,128]{1,0:T(8,128)(2,1)}, bf16[2192,128]{1,0:T(8,128)(2,1)S(1)}, u32[]{:S(2)}, u32[]{:S(2)}) collective-permute-start(bf16[2192,128]{1,0:T(8,128)(2,1)} %get-tuple-element.15.q_ref), channel_id=1, source_target_pairs={{2,0},{3,1},{4,2},{5,3},{6,4},{7,5},{8,6},{9,7},{10,8},{11,9},{12,... | collective-permute-start | bytes 1683464 | tf_op jit(solution)/shard_map/ppermute | solution.py:301
  12.0 12.7 %collective-permute-start.4 = (bf16[2192,128]{1,0:T(8,128)(2,1)}, bf16[2192,128]{1,0:T(8,128)(2,1)}, u32[]{:S(2)}, u32[]{:S(2)}) collective-permute-start(bf16[2192,128]{1,0:T(8,128)(2,1)} %get-tuple-element.15.q_ref), channel_id=1, source_target_pairs={{1,1},{3,3},{4,0},{5,5},{6,2},{7,7},{8,4},{9,9},{10,6},{11,11},{12... | collective-permute-start | bytes 1683464 | tf_op jit(solution)/shard_map/ppermute | solution.py:301
  24.6 0.1 pad_add_fusion.flags
  24.7 4.1 %attend_own.1.own_ref = bf16[2240,128]{1,0:T(8,128)(2,1)S(1)} custom-call(s32[2]{0:T(128)S(1)} %pad_add_fusion.flags, bf16[2192,128]{1,0:T(8,128)(2,1)} %get-tuple-element.15.q_ref, bf16[2,8,512,128]{3,2,1,0:T(8,128)(2,1)S(1)} %pad_maximum_fusion.refs_0_, f32[24,128]{1,0:T(8,128)S(1)} %get-tuple-element.16.refs_1_), custom_call_target="tpu_custom_call" | custom-call | flops 1000 | bytes 1000 | tf_op jit(solution)/shard_map/attend_own/pallas_call | solution.py:207
  28.9 0.0 collective-permute-done.q_ref
  28.9 0.0 collective-permute-done.1.refs_1_
  28.9 0.0 collective-permute-done.2.refs_2_
  28.9 6.1 %attend_near.1 = bf16[2240,128]{1,0:T(8,128)(2,1)} custom-call(s32[2]{0:T(128)S(1)} %pad_add_fusion.flags, bf16[2192,128]{1,0:T(8,128)(2,1)S(1)} %collective-permute-done.q_ref, bf16[2,8,512,128]{3,2,1,0:T(8,128)(2,1)S(1)} %pad_maximum_fusion.refs_0_, bf16[2,8,512,128]{3,2,1,0:T(8,128)(2,1)} %collective-permute-done.1.refs_1_, ...), custom_call_target="tpu_custom_call" | custom-call | flops 1000 | bytes 1000 | tf_op jit(solution)/shard_map/attend_near/pallas_call | solution.py:207
  35.0 3.6 %collective-permute-start.3 = (bf16[2240,128]{1,0:T(8,128)(2,1)}, bf16[2240,128]{1,0:T(8,128)(2,1)}, u32[]{:S(2)}, u32[]{:S(2)}) collective-permute-start(bf16[2240,128]{1,0:T(8,128)(2,1)} %attend_near.1), channel_id=1, source_target_pairs={{0,2},{1,3},{2,4},{3,5},{4,6},{5,7},{6,8},{7,9},{8,10},{9,11},{10,... | collective-permute-start | bytes 1720328 | tf_op jit(solution)/shard_map/ppermute | solution.py:301
  38.6 0.0 collective-permute-done.4.q_ref
  38.6 5.2 %attend_far.1.here_ref = bf16[2240,128]{1,0:T(8,128)(2,1)S(1)} custom-call(s32[2]{0:T(128)S(1)} %pad_add_fusion.flags, bf16[2192,128]{1,0:T(8,128)(2,1)} %collective-permute-done.4.q_ref, bf16[2,8,512,128]{3,2,1,0:T(8,128)(2,1)S(1)} %pad_maximum_fusion.refs_0_, bf16[2,8,512,128]{3,2,1,0:T(8,128)(2,1)} %collective-permute-done.1.refs_1_), custom_call_target="tpu_custom_call" | custom-call | flops 1000 | bytes 1000 | tf_op jit(solution)/shard_map/attend_far/pallas_call | solution.py:207
  43.8 6.4 %collective-permute-start.5 = (bf16[2240,128]{1,0:T(8,128)(2,1)S(1)}, bf16[2240,128]{1,0:T(8,128)(2,1)S(1)}, u32[]{:S(2)}, u32[]{:S(2)}) collective-permute-start(bf16[2240,128]{1,0:T(8,128)(2,1)S(1)} %attend_far.1.here_ref), channel_id=1, source_target_pairs={{0,4},{2,6},{4,8},{6,10},{8,12},{10,14},{12,16},{14,18},{16,20},{1... | collective-permute-start | bytes 1720328 | tf_op jit(solution)/shard_map/ppermute | solution.py:301
  50.2 0.1 copy.12
  50.3 0.3 reshape.12.slots_ref
  50.6 12.6 %collective-permute-done.3.back_ref.near_ref = bf16[2240,128]{1,0:T(8,128)(2,1)} collective-permute-done((bf16[2240,128]{1,0:T(8,128)(2,1)}, bf16[2240,128]{1,0:T(8,128)(2,1)}, u32[]{:S(2)}, u32[]{:S(2)}) %collective-permute-start.3) | collective-permute-done | bytes 573472 | tf_op jit(solution)/shard_map/ppermute | solution.py:301
  63.2 1.5 %mix_early.1 = (bf16[2176,128]{1,0:T(8,128)(2,1)S(1)}, f32[24,128]{1,0:T(8,128)S(1)}) custom-call(s32[2]{0:T(128)S(1)} %pad_add_fusion.flags, bf16[2240,128]{1,0:T(8,128)(2,1)S(1)} %attend_own.1.own_ref, bf16[2240,128]{1,0:T(8,128)(2,1)} %collective-permute-done.3.back_ref.near_ref, bf16[2240,128]{1,0:T(8,128)(2,1)S(1)} %attend_far.1.here_ref), custom_call_target="tpu_custom_call" | custom-call | flops 1000 | bytes 1000 | tf_op jit(solution)/shard_map/mix_early/pallas_call | solution.py:255
  64.7 18.5 %collective-permute-done.5.far_ref = bf16[2240,128]{1,0:T(8,128)(2,1)S(1)} collective-permute-done((bf16[2240,128]{1,0:T(8,128)(2,1)S(1)}, bf16[2240,128]{1,0:T(8,128)(2,1)S(1)}, u32[]{:S(2)}, u32[]{:S(2)}) %collective-permute-start.5) | collective-permute-done | bytes 573472 | tf_op jit(solution)/shard_map/ppermute | solution.py:301
  83.2 4.8 %finish.1 = bf16[2048,128]{1,0:T(8,128)(2,1)} custom-call(s32[2]{0:T(128)S(1)} %pad_add_fusion.flags, bf16[2176,128]{1,0:T(8,128)(2,1)S(1)} %get-tuple-element.19.sum_ref, f32[24,128]{1,0:T(8,128)S(1)} %get-tuple-element.20.lines_ref, bf16[2240,128]{1,0:T(8,128)(2,1)} %collective-permute-done.3.back_ref.near_ref, ...), custom_call_target="tpu_custom_call" | custom-call | flops 1000 | bytes 1000 | tf_op jit(solution)/shard_map/finish/pallas_call | solution.py:287
Async XLA Ops:
  1.9 4.2 %copy-start.1 = (bf16[256,8,128]{2,1,0:T(8,128)(2,1)S(1)}, bf16[256,8,128]{2,1,0:T(8,128)(2,1)}, u32[]{:S(2)}) copy-start(bf16[256,8,128]{2,1,0:T(8,128)(2,1)} %param.4) | copy-start | bytes 1572868
  1.9 4.2 %copy-start = (s32[256,8]{0,1:T(8,128)S(1)}, s32[256,8]{0,1:T(8,128)}, u32[]{:S(2)}) copy-start(s32[256,8]{0,1:T(8,128)} %param.7) | copy-start | bytes 24580
  2.2 26.7 %collective-permute-start.1 = (bf16[2,8,512,128]{3,2,1,0:T(8,128)(2,1)S(1)}, bf16[2,8,512,128]{3,2,1,0:T(8,128)(2,1)}, u32[]{:S(2)}, u32[]{:S(2)}) collective-permute-start(bf16[2,8,512,128]{3,2,1,0:T(8,128)(2,1)S(1)} %pad_maximum_fusion.refs_0_), channel_id=1, source_target_pairs={{0,1},{1,0},{2,3},{3,2},{4,5},{5,4},{6,7},{7,6},{8,9},{9,8},{10,11... | collective-permute-start | bytes 6291464 | tf_op jit(solution)/shard_map/ppermute | solution.py:301
  4.1 24.8 %collective-permute-start.2 = (bf16[2,8,512,128]{3,2,1,0:T(8,128)(2,1)S(1)}, bf16[2,8,512,128]{3,2,1,0:T(8,128)(2,1)}, u32[]{:S(2)}, u32[]{:S(2)}) collective-permute-start(bf16[2,8,512,128]{3,2,1,0:T(8,128)(2,1)S(1)} %pad_maximum_fusion.refs_0_), channel_id=1, source_target_pairs={{1,3},{3,5},{5,7},{7,9},{9,11},{11,13},{13,15},{15,17},{17,19},{19... | collective-permute-start | bytes 6291464 | tf_op jit(solution)/shard_map/ppermute | solution.py:301
  10.0 18.8 %collective-permute-start = (bf16[2192,128]{1,0:T(8,128)(2,1)}, bf16[2192,128]{1,0:T(8,128)(2,1)S(1)}, u32[]{:S(2)}, u32[]{:S(2)}) collective-permute-start(bf16[2192,128]{1,0:T(8,128)(2,1)} %get-tuple-element.15.q_ref), channel_id=1, source_target_pairs={{2,0},{3,1},{4,2},{5,3},{6,4},{7,5},{8,6},{9,7},{10,8},{11,9},{12,... | collective-permute-start | bytes 1683464 | tf_op jit(solution)/shard_map/ppermute | solution.py:301
  12.0 26.6 %collective-permute-start.4 = (bf16[2192,128]{1,0:T(8,128)(2,1)}, bf16[2192,128]{1,0:T(8,128)(2,1)}, u32[]{:S(2)}, u32[]{:S(2)}) collective-permute-start(bf16[2192,128]{1,0:T(8,128)(2,1)} %get-tuple-element.15.q_ref), channel_id=1, source_target_pairs={{1,1},{3,3},{4,0},{5,5},{6,2},{7,7},{8,4},{9,9},{10,6},{11,11},{12... | collective-permute-start | bytes 1683464 | tf_op jit(solution)/shard_map/ppermute | solution.py:301
  35.0 28.2 %collective-permute-start.3 = (bf16[2240,128]{1,0:T(8,128)(2,1)}, bf16[2240,128]{1,0:T(8,128)(2,1)}, u32[]{:S(2)}, u32[]{:S(2)}) collective-permute-start(bf16[2240,128]{1,0:T(8,128)(2,1)} %attend_near.1), channel_id=1, source_target_pairs={{0,2},{1,3},{2,4},{3,5},{4,6},{5,7},{6,8},{7,9},{8,10},{9,11},{10,... | collective-permute-start | bytes 1720328 | tf_op jit(solution)/shard_map/ppermute | solution.py:301
  43.8 39.4 %collective-permute-start.5 = (bf16[2240,128]{1,0:T(8,128)(2,1)S(1)}, bf16[2240,128]{1,0:T(8,128)(2,1)S(1)}, u32[]{:S(2)}, u32[]{:S(2)}) collective-permute-start(bf16[2240,128]{1,0:T(8,128)(2,1)S(1)} %attend_far.1.here_ref), channel_id=1, source_target_pairs={{0,4},{2,6},{4,8},{6,10},{8,12},{10,14},{12,16},{14,18},{16,20},{1... | collective-permute-start | bytes 1720328 | tf_op jit(solution)/shard_map/ppermute | solution.py:301

commit v7 on v4

--- a/solution.py
+++ b/solution.py
@@ -16,8 +16,8 @@
 BLOCKS = ROWS // 128
 LINES = 24
 CHUNK = 160
-STEP = 4
-LIMIT = 32 * 2**20
+STEP = 8
+LIMIT = 44 * 2**20
 SMALL = pl.CostEstimate(flops=1000, bytes_accessed=1000, transcendentals=0)
 LOW = -1e30
 SCALE = 1.4426950408889634 / (128.0**0.5)

time: 86.4 us -> 87.3 us (1.010)
  the two profiles are of different devices: /device:TPU:120 before, /device:TPU:112 now
where the time goes in v7:
time: 87.3 us; the launch traced here: 86.8 us
  waiting for transfers between devices  30.1 us (34%)
  starting transfers between devices  27.3 us (31%)
  Pallas kernels  26.3 us (30%)
  local copies, waits for them, and re-layouts  2.61 us (3%)
    ppermute x6, waiting for transfers between devices, moved(): return lax.ppermute(block, 'seq', pairs)  30.1 us
    ppermute x6, starting transfers between devices, moved(): return lax.ppermute(block, 'seq', pairs)  27.3 us
    pallas_call x3, Pallas kernels, attend(): pl.pallas_call(functools.partial(attend_kernel, kind), grid=(GROUPS // ST...  16 us
    pallas_call x1, Pallas kernels, finish(): pl.pallas_call(finish_kernel, in_specs=[pl.BlockSpec(memory_space=pltpu.S...  5.02 us
    pallas_call x1, Pallas kernels, sort_queries(): pl.pallas_call(sort_kernel, out_shape=[jax.ShapeDtypeStruct((ROWS + META,...  3.85 us
    another operation x1, local copies, waits for them, and re-layouts, shards(): kv = jnp.stack([keys.transpose(1, 0, 2), values.transpose(1, 0, 2)])  1.92 us
  transfers between devices with their start and end apart: 6, of which 3 were waited for; matrix products, arithmetic and copies ran while one was open for 1% of the time, Pallas kernels for 25%

profile of v7, /device:TPU:112, one launch (start us, length us, event | category | flops | bytes accessed | tf_op | source)
XLA Modules:
  0.0 86.8 jit_solution(12970372905347818642)
XLA Ops:
  0.0 1.9 %copy_bitcast_fusion = (bf16[1,8,512,128]{3,2,1,0:T(8,128)(2,1)S(1)}, bf16[1,8,512,128]{3,2,1,0:T(8,128)(2,1)S(1)}) fusion(bf16[512,8,128]{2,1,0:T(8,128)(2,1)} %param.6, bf16[512,8,128]{2,1,0:T(8,128)(2,1)} %param.5), kind=kLoop, calls=%fused_computation.1 | loop fusion | bytes 4194304 | tf_op jit(solution)/shard_map/stack | solution.py:313
  1.9 0.0 copy-start.1
  1.9 0.0 copy-start
  2.0 0.2 pad_maximum_fusion.refs_0_
  2.2 1.9 %collective-permute-start.1 = (bf16[2,8,512,128]{3,2,1,0:T(8,128)(2,1)S(1)}, bf16[2,8,512,128]{3,2,1,0:T(8,128)(2,1)}, u32[]{:S(2)}, u32[]{:S(2)}) collective-permute-start(bf16[2,8,512,128]{3,2,1,0:T(8,128)(2,1)S(1)} %pad_maximum_fusion.refs_0_), channel_id=1, source_target_pairs={{0,1},{1,0},{2,3},{3,2},{4,5},{5,4},{6,7},{7,6},{8,9},{9,8},{10,11... | collective-permute-start | bytes 6291464 | tf_op jit(solution)/shard_map/ppermute | solution.py:301
  4.1 2.0 %collective-permute-start.2 = (bf16[2,8,512,128]{3,2,1,0:T(8,128)(2,1)S(1)}, bf16[2,8,512,128]{3,2,1,0:T(8,128)(2,1)}, u32[]{:S(2)}, u32[]{:S(2)}) collective-permute-start(bf16[2,8,512,128]{3,2,1,0:T(8,128)(2,1)S(1)} %pad_maximum_fusion.refs_0_), channel_id=1, source_target_pairs={{1,3},{3,5},{5,7},{7,9},{9,11},{11,13},{13,15},{15,17},{17,19},{19... | collective-permute-start | bytes 6291464 | tf_op jit(solution)/shard_map/ppermute | solution.py:301
  6.1 0.0 copy-done.1
  6.1 0.1 copy.11
  6.2 0.0 copy-done
  6.2 3.9 %sort_queries.1 = (bf16[2192,128]{1,0:T(8,128)(2,1)}, f32[24,128]{1,0:T(8,128)S(1)}, s32[8,256]{1,0:T(8,128)S(1)}) custom-call(s32[8,256]{1,0:T(8,128)S(1)} %bitcast.16, bf16[2048,128]{1,0:T(8,128)(2,1)S(1)} %bitcast.15), custom_call_target="tpu_custom_call" | custom-call | flops 1000 | bytes 1000 | tf_op jit(solution)/shard_map/sort_queries/pallas_call | solution.py:77
  10.0 1.9 %collective-permute-start = (bf16[2192,128]{1,0:T(8,128)(2,1)}, bf16[2192,128]{1,0:T(8,128)(2,1)S(1)}, u32[]{:S(2)}, u32[]{:S(2)}) collective-permute-start(bf16[2192,128]{1,0:T(8,128)(2,1)} %get-tuple-element.20.q_ref), channel_id=1, source_target_pairs={{2,0},{3,1},{4,2},{5,3},{6,4},{7,5},{8,6},{9,7},{10,8},{11,9},{12,... | collective-permute-start | bytes 1683464 | tf_op jit(solution)/shard_map/ppermute | solution.py:301
  11.9 0.1 pad_add_fusion.flags
  12.0 4.1 %attend_own.1.own_ref = bf16[2240,128]{1,0:T(8,128)(2,1)S(1)} custom-call(s32[2]{0:T(128)S(1)} %pad_add_fusion.flags, bf16[2192,128]{1,0:T(8,128)(2,1)} %get-tuple-element.20.q_ref, bf16[2,8,512,128]{3,2,1,0:T(8,128)(2,1)S(1)} %pad_maximum_fusion.refs_0_, f32[24,128]{1,0:T(8,128)S(1)} %get-tuple-element.17.refs_1_), custom_call_target="tpu_custom_call" | custom-call | flops 1000 | bytes 1000 | tf_op jit(solution)/shard_map/attend_own/pallas_call | solution.py:207
  16.1 0.1 copy.12
  16.3 0.1 reshape.10
  16.4 13.6 %collective-permute-start.4 = (bf16[2192,128]{1,0:T(8,128)(2,1)}, bf16[2192,128]{1,0:T(8,128)(2,1)S(1)}, u32[]{:S(2)}, u32[]{:S(2)}) collective-permute-start(bf16[2192,128]{1,0:T(8,128)(2,1)} %get-tuple-element.20.q_ref), channel_id=1, source_target_pairs={{1,1},{3,3},{4,0},{5,5},{6,2},{7,7},{8,4},{9,9},{10,6},{11,11},{12... | collective-permute-start | bytes 1683464 | tf_op jit(solution)/shard_map/ppermute | solution.py:301
  30.0 0.0 collective-permute-done.q_ref
  30.0 0.0 collective-permute-done.1.refs_1_
  30.0 0.0 collective-permute-done.2.refs_2_
  30.0 6.8 %attend_near.1 = bf16[2240,128]{1,0:T(8,128)(2,1)} custom-call(s32[2]{0:T(128)S(1)} %pad_add_fusion.flags, bf16[2192,128]{1,0:T(8,128)(2,1)S(1)} %collective-permute-done.q_ref, bf16[2,8,512,128]{3,2,1,0:T(8,128)(2,1)S(1)} %pad_maximum_fusion.refs_0_, bf16[2,8,512,128]{3,2,1,0:T(8,128)(2,1)} %collective-permute-done.1.refs_1_, ...), custom_call_target="tpu_custom_call" | custom-call | flops 1000 | bytes 1000 | tf_op jit(solution)/shard_map/attend_near/pallas_call | solution.py:207
  36.8 3.4 %collective-permute-start.3 = (bf16[2240,128]{1,0:T(8,128)(2,1)}, bf16[2240,128]{1,0:T(8,128)(2,1)}, u32[]{:S(2)}, u32[]{:S(2)}) collective-permute-start(bf16[2240,128]{1,0:T(8,128)(2,1)} %attend_near.1), channel_id=1, source_target_pairs={{0,2},{1,3},{2,4},{3,5},{4,6},{5,7},{6,8},{7,9},{8,10},{9,11},{10,... | collective-permute-start | bytes 1720328 | tf_op jit(solution)/shard_map/ppermute | solution.py:301
  40.1 0.8 collective-permute-done.4.q_ref
  40.9 5.1 %attend_far.1.here_ref = bf16[2240,128]{1,0:T(8,128)(2,1)S(1)} custom-call(s32[2]{0:T(128)S(1)} %pad_add_fusion.flags, bf16[2192,128]{1,0:T(8,128)(2,1)S(1)} %collective-permute-done.4.q_ref, bf16[2,8,512,128]{3,2,1,0:T(8,128)(2,1)S(1)} %pad_maximum_fusion.refs_0_, bf16[2,8,512,128]{3,2,1,0:T(8,128)(2,1)} %collective-permute-done.1.refs_1_), custom_call_target="tpu_custom_call" | custom-call | flops 1000 | bytes 1000 | tf_op jit(solution)/shard_map/attend_far/pallas_call | solution.py:207
  46.1 4.5 %collective-permute-start.5 = (bf16[2240,128]{1,0:T(8,128)(2,1)S(1)}, bf16[2240,128]{1,0:T(8,128)(2,1)S(1)}, u32[]{:S(2)}, u32[]{:S(2)}) collective-permute-start(bf16[2240,128]{1,0:T(8,128)(2,1)S(1)} %attend_far.1.here_ref), channel_id=1, source_target_pairs={{0,4},{2,6},{4,8},{6,10},{8,12},{10,14},{12,16},{14,18},{16,20},{1... | collective-permute-start | bytes 1720328 | tf_op jit(solution)/shard_map/ppermute | solution.py:301
  50.6 0.4 copy.13.slots_ref
  51.0 8.6 %collective-permute-done.3.back_ref.near_ref = bf16[2240,128]{1,0:T(8,128)(2,1)} collective-permute-done((bf16[2240,128]{1,0:T(8,128)(2,1)}, bf16[2240,128]{1,0:T(8,128)(2,1)}, u32[]{:S(2)}, u32[]{:S(2)}) %collective-permute-start.3) | collective-permute-done | bytes 573472 | tf_op jit(solution)/shard_map/ppermute | solution.py:301
  59.6 1.5 %mix_early.1 = (bf16[2176,128]{1,0:T(8,128)(2,1)S(1)}, f32[24,128]{1,0:T(8,128)S(1)}) custom-call(s32[2]{0:T(128)S(1)} %pad_add_fusion.flags, bf16[2240,128]{1,0:T(8,128)(2,1)S(1)} %attend_own.1.own_ref, bf16[2240,128]{1,0:T(8,128)(2,1)} %collective-permute-done.3.back_ref.near_ref, bf16[2240,128]{1,0:T(8,128)(2,1)S(1)} %attend_far.1.here_ref), custom_call_target="tpu_custom_call" | custom-call | flops 1000 | bytes 1000 | tf_op jit(solution)/shard_map/mix_early/pallas_call | solution.py:255
  61.1 20.7 %collective-permute-done.5.far_ref = bf16[2240,128]{1,0:T(8,128)(2,1)S(1)} collective-permute-done((bf16[2240,128]{1,0:T(8,128)(2,1)S(1)}, bf16[2240,128]{1,0:T(8,128)(2,1)S(1)}, u32[]{:S(2)}, u32[]{:S(2)}) %collective-permute-start.5) | collective-permute-done | bytes 573472 | tf_op jit(solution)/shard_map/ppermute | solution.py:301
  81.8 5.0 %finish.1 = bf16[2048,128]{1,0:T(8,128)(2,1)} custom-call(s32[2]{0:T(128)S(1)} %pad_add_fusion.flags, bf16[2176,128]{1,0:T(8,128)(2,1)S(1)} %get-tuple-element.22.sum_ref, f32[24,128]{1,0:T(8,128)S(1)} %get-tuple-element.23.lines_ref, bf16[2240,128]{1,0:T(8,128)(2,1)} %collective-permute-done.3.back_ref.near_ref, ...), custom_call_target="tpu_custom_call" | custom-call | flops 1000 | bytes 1000 | tf_op jit(solution)/shard_map/finish/pallas_call | solution.py:287
Async XLA Ops:
  1.9 4.2 %copy-start.1 = (bf16[256,8,128]{2,1,0:T(8,128)(2,1)S(1)}, bf16[256,8,128]{2,1,0:T(8,128)(2,1)}, u32[]{:S(2)}) copy-start(bf16[256,8,128]{2,1,0:T(8,128)(2,1)} %param.4) | copy-start | bytes 1572868
  1.9 4.2 %copy-start = (s32[256,8]{0,1:T(8,128)S(1)}, s32[256,8]{0,1:T(8,128)}, u32[]{:S(2)}) copy-start(s32[256,8]{0,1:T(8,128)} %param.7) | copy-start | bytes 24580
  2.2 27.8 %collective-permute-start.1 = (bf16[2,8,512,128]{3,2,1,0:T(8,128)(2,1)S(1)}, bf16[2,8,512,128]{3,2,1,0:T(8,128)(2,1)}, u32[]{:S(2)}, u32[]{:S(2)}) collective-permute-start(bf16[2,8,512,128]{3,2,1,0:T(8,128)(2,1)S(1)} %pad_maximum_fusion.refs_0_), channel_id=1, source_target_pairs={{0,1},{1,0},{2,3},{3,2},{4,5},{5,4},{6,7},{7,6},{8,9},{9,8},{10,11... | collective-permute-start | bytes 6291464 | tf_op jit(solution)/shard_map/ppermute | solution.py:301
  4.1 25.9 %collective-permute-start.2 = (bf16[2,8,512,128]{3,2,1,0:T(8,128)(2,1)S(1)}, bf16[2,8,512,128]{3,2,1,0:T(8,128)(2,1)}, u32[]{:S(2)}, u32[]{:S(2)}) collective-permute-start(bf16[2,8,512,128]{3,2,1,0:T(8,128)(2,1)S(1)} %pad_maximum_fusion.refs_0_), channel_id=1, source_target_pairs={{1,3},{3,5},{5,7},{7,9},{9,11},{11,13},{13,15},{15,17},{17,19},{19... | collective-permute-start | bytes 6291464 | tf_op jit(solution)/shard_map/ppermute | solution.py:301
  10.0 20.0 %collective-permute-start = (bf16[2192,128]{1,0:T(8,128)(2,1)}, bf16[2192,128]{1,0:T(8,128)(2,1)S(1)}, u32[]{:S(2)}, u32[]{:S(2)}) collective-permute-start(bf16[2192,128]{1,0:T(8,128)(2,1)} %get-tuple-element.20.q_ref), channel_id=1, source_target_pairs={{2,0},{3,1},{4,2},{5,3},{6,4},{7,5},{8,6},{9,7},{10,8},{11,9},{12,... | collective-permute-start | bytes 1683464 | tf_op jit(solution)/shard_map/ppermute | solution.py:301
  16.4 24.5 %collective-permute-start.4 = (bf16[2192,128]{1,0:T(8,128)(2,1)}, bf16[2192,128]{1,0:T(8,128)(2,1)S(1)}, u32[]{:S(2)}, u32[]{:S(2)}) collective-permute-start(bf16[2192,128]{1,0:T(8,128)(2,1)} %get-tuple-element.20.q_ref), channel_id=1, source_target_pairs={{1,1},{3,3},{4,0},{5,5},{6,2},{7,7},{8,4},{9,9},{10,6},{11,11},{12... | collective-permute-start | bytes 1683464 | tf_op jit(solution)/shard_map/ppermute | solution.py:301
  36.8 22.8 %collective-permute-start.3 = (bf16[2240,128]{1,0:T(8,128)(2,1)}, bf16[2240,128]{1,0:T(8,128)(2,1)}, u32[]{:S(2)}, u32[]{:S(2)}) collective-permute-start(bf16[2240,128]{1,0:T(8,128)(2,1)} %attend_near.1), channel_id=1, source_target_pairs={{0,2},{1,3},{2,4},{3,5},{4,6},{5,7},{6,8},{7,9},{8,10},{9,11},{10,... | collective-permute-start | bytes 1720328 | tf_op jit(solution)/shard_map/ppermute | solution.py:301
  46.1 35.7 %collective-permute-start.5 = (bf16[2240,128]{1,0:T(8,128)(2,1)S(1)}, bf16[2240,128]{1,0:T(8,128)(2,1)S(1)}, u32[]{:S(2)}, u32[]{:S(2)}) collective-permute-start(bf16[2240,128]{1,0:T(8,128)(2,1)S(1)} %attend_far.1.here_ref), channel_id=1, source_target_pairs={{0,4},{2,6},{4,8},{6,10},{8,12},{10,14},{12,16},{14,18},{16,20},{1... | collective-permute-start | bytes 1720328 | tf_op jit(solution)/shard_map/ppermute | solution.py:301
